TPU v7x, 256 devices: a whole 4x4x8 slice. The times are simulated.
256 devices in a mesh: seq: 8 (over y_lo, x), expert: 32 (over z, y_hi, core).
Axes of the slice: x: 4, y: 4 (y_hi: 2, y_lo: 2; y = y_hi * 2 + y_lo), z: 8, core: 2. Of those that a mesh axis runs over, the one named last changes fastest.
Arguments:
- tokens: bfloat16 [32768, 4096], P(('seq', 'expert')), may hold values from -40 to 40
- slot_keys: bfloat16 [64, 4096], P('expert'), may hold values from -12 to 12
- w_in: bfloat16 [32, 4096, 2048], P('expert', None, 'seq'), may hold values from -0.09375 to 0.09375
- w_out: bfloat16 [32, 2048, 4096], P('expert', 'seq'), may hold values from -0.125 to 0.125
- cotangent: bfloat16 [32768, 4096], P(('seq', 'expert')), may hold values from -6 to 6
Outputs:
- layer_out: bfloat16 [32768, 4096], P(('seq', 'expert'))
- token_grad: bfloat16 [32768, 4096], P(('seq', 'expert'))
- key_grad: float32 [64, 4096], P('expert')
- w_in_grad: bfloat16 [32, 4096, 2048], P('expert', None, 'seq')
- w_out_grad: bfloat16 [32, 2048, 4096], P('expert', 'seq')
All inputs are finite; a program needn't handle non-finite values.
Results may differ from a plain program's by a relative error of at most 0.03.
Values may be sent and summed in bfloat16 or wider, within the bound.
No kernel may reach another device: no remote copies, remote signals or barrier semaphores. Data moves between devices by JAX's collectives and lax.ppermute only.
A program may use at most 64 MiB of HBM per device.

v0:
```python
import jax
import jax.numpy as jnp
from jax import lax
from jax.sharding import PartitionSpec as P


def gelu_tanh(values):
    return jax.nn.gelu(values, approximate=True)


def body(tokens, slot_keys, w_in, w_out, cotangent):
    rows_local = slot_keys.shape[0]
    model_width = tokens.shape[1]
    experts_here = w_in.shape[0]
    keys_all = lax.all_gather(slot_keys, "expert", axis=0, tiled=True)
    logits = jnp.einsum("jd,td->jt", keys_all, tokens, preferred_element_type=jnp.float32)
    col_peak = jnp.max(logits, axis=0, keepdims=True)
    col_exp = jnp.exp(logits - col_peak)
    combine = (col_exp / jnp.sum(col_exp, axis=0, keepdims=True)).astype(jnp.bfloat16)
    combine_wide = combine.astype(jnp.float32)
    local_peak = jnp.max(logits, axis=1)
    peak_max = lax.pmax(local_peak, ("seq", "expert"))
    row_exp = jnp.exp(logits - peak_max[:, None])
    totals = lax.psum(jnp.sum(row_exp, axis=1), ("seq", "expert"))
    dispatch = (row_exp / totals[:, None]).astype(jnp.bfloat16)
    dispatch_wide = dispatch.astype(jnp.float32)
    weights = dispatch
    slot_sum = lax.psum(
        lax.psum_scatter(
            jnp.dot(weights, tokens, preferred_element_type=jnp.float32),
            "expert",
            scatter_dimension=0,
            tiled=True,
        ),
        "seq",
    )
    slot_in = slot_sum.astype(jnp.bfloat16).reshape(experts_here, -1, model_width)
    pre_act = jnp.einsum("esd,edf->esf", slot_in, w_in, preferred_element_type=jnp.float32)
    hidden_act = gelu_tanh(pre_act).astype(jnp.bfloat16)
    partial_out = jnp.einsum("esf,efd->esd", hidden_act, w_out, preferred_element_type=jnp.float32)
    expert_out = lax.psum(partial_out, "seq")
    out_rows = expert_out.reshape(rows_local, model_width).astype(jnp.bfloat16)
    portion = lax.all_gather(out_rows, "expert", axis=0, tiled=True)
    weights = combine
    mixed_acc = jnp.einsum("jt,jd->td", weights, portion, preferred_element_type=jnp.float32)
    dots = jnp.einsum("jd,td->jt", portion, cotangent, preferred_element_type=jnp.float32)
    combine_dot = dots
    mixed_acc, combine_dot = (mixed_acc, combine_dot)
    layer_out = mixed_acc.astype(jnp.bfloat16)
    combine_grad = combine_wide * (
        combine_dot - jnp.sum(combine_wide * combine_dot, axis=0, keepdims=True)
    )
    weights = combine
    out_sum = lax.psum(
        lax.psum_scatter(
            jnp.dot(weights, cotangent, preferred_element_type=jnp.float32),
            "expert",
            scatter_dimension=0,
            tiled=True,
        ),
        "seq",
    )
    out_grad = out_sum.astype(jnp.bfloat16).reshape(experts_here, -1, model_width)
    w_out_grad = jnp.einsum(
        "esf,esd->efd", hidden_act, out_grad, preferred_element_type=jnp.float32
    ).astype(jnp.bfloat16)
    act_grad = jnp.einsum("esd,efd->esf", out_grad, w_out, preferred_element_type=jnp.float32)
    _, pullback = jax.vjp(gelu_tanh, pre_act)
    pre_grad = pullback(act_grad)[0].astype(jnp.bfloat16)
    w_in_grad = jnp.einsum(
        "esd,esf->edf", slot_in, pre_grad, preferred_element_type=jnp.float32
    ).astype(jnp.bfloat16)
    slot_part = jnp.einsum("esf,edf->esd", pre_grad, w_in, preferred_element_type=jnp.float32)
    slot_grad = lax.psum(slot_part, "seq").reshape(rows_local, model_width).astype(jnp.bfloat16)
    portion = lax.all_gather(slot_grad, "expert", axis=0, tiled=True)
    dots = jnp.einsum("jd,td->jt", portion, tokens, preferred_element_type=jnp.float32)
    pick_grad = dots
    weights = dispatch
    token_acc = jnp.einsum("jt,jd->td", weights, portion, preferred_element_type=jnp.float32)
    pick_grad, token_acc = (pick_grad, token_acc)
    crossing = lax.psum(jnp.sum(dispatch_wide * pick_grad, axis=1), ("seq", "expert"))
    logit_grad = (dispatch_wide * (pick_grad - crossing[:, None]) + combine_grad).astype(
        jnp.bfloat16
    )
    token_grad = (
        token_acc
        + jnp.einsum("jt,jd->td", logit_grad, keys_all, preferred_element_type=jnp.float32)
    ).astype(jnp.bfloat16)
    weights = logit_grad
    key_grad = lax.psum(
        lax.psum_scatter(
            jnp.dot(weights, tokens, preferred_element_type=jnp.float32),
            "expert",
            scatter_dimension=0,
            tiled=True,
        ),
        "seq",
    )
    return (layer_out, token_grad, key_grad, w_in_grad, w_out_grad)


def solution(mesh):
    in_specs = (
        P(("seq", "expert"), None),
        P("expert", None),
        P("expert", None, "seq"),
        P("expert", "seq", None),
        P(("seq", "expert"), None),
    )
    out_specs = (
        P(("seq", "expert"), None),
        P(("seq", "expert"), None),
        P("expert", None),
        P("expert", None, "seq"),
        P("expert", "seq", None),
    )
    return jax.shard_map(body, mesh=mesh, in_specs=in_specs, out_specs=out_specs, check_vma=False)
```

profile of v0, /device:TPU:2, one launch (start us, length us, event | category | flops | bytes accessed | tf_op | source)
XLA Modules:
  0.0 1020.9 jit_solution(14672386643014092537)
XLA Ops:
  7.2 0.0 copy-start
  7.2 0.0 copy-start.1
  7.2 0.0 all-reduce.11.cloned.1.call-start
  7.2 49.3 %all-gather.2 = bf16[32,2,4096]{2,1,0:T(2,128)(2,1)} all-gather(bf16[1,2,4096]{2,1,0:T(2,128)(2,1)} %bitcast.58), channel_id=1, replica_groups=mesh['seq'=8,'expert'=32] {'expert'}, dimensions={0}, use_global_device_ids=true | all-gather | bytes 540672 | tf_op jit(solution)/shard_map/all_gather | solution.py:15
  56.6 2.0 reshape.82
  58.6 2.0 fusion.45
  60.6 73.9 %pmax.7 = f32[64]{0:T(128)S(1)} all-reduce(f32[64]{0:T(128)S(1)} %get-tuple-element.7), channel_id=1, replica_groups=mesh['seq'=8,'expert'=32] {'seq','expert'}, use_global_device_ids=true, to_apply=%region_3.0 | all-reduce | flops 64 | bytes 512 | tf_op jit(solution)/shard_map/pmax | solution.py:22
  134.5 0.2 fusion.25
  134.7 74.3 %psum.49 = f32[64]{0:T(128)S(1)} all-reduce(f32[64]{0:T(128)S(1)} %get-tuple-element.5), channel_id=1, replica_groups=mesh['seq'=8,'expert'=32] {'seq','expert'}, use_global_device_ids=true, to_apply=%region_5.0 | all-reduce | flops 64 | bytes 512 | tf_op jit(solution)/shard_map/psum | solution.py:24
  209.0 0.1 divide_convert_fusion
  209.1 0.0 copy-done.1
  209.1 1.3 fusion.46
  210.3 0.0 copy-done.4
  210.4 1.3 fusion.47
  211.6 0.0 all-reduce.11.cloned.1.call-update
  211.6 0.0 all-reduce.9.cloned.1.call-start
  211.7 0.0 copy-done.9
  211.7 0.6 dynamic-slice
  212.9 268.5 %all-reduce.11.cloned.1.call-done = (f32[64,4096]{1,0:T(8,128)}, f32[64,4096]{1,0:T(8,128)}) async-done(((f32[64,4096]{1,0:T(8,128)}, f32[64,4096]{1,0:T(8,128)}), (f32[64,4096]{1,0:T(8,128)}, f32[64,4096]{1,0:T(8,128)})) %all-reduce.11.cloned.1.call-update) | async-done | bytes 2097168
  481.4 1.0 constant_dynamic-slice_fusion.1
  482.4 29.9 %all-reduce.5 = (bf16[2,4096]{1,0:T(2,128)(2,1)S(1)}, bf16[2,4096]{1,0:T(2,128)(2,1)S(1)}) all-reduce(f32[2,4096]{1,0:T(2,128)S(1)} %get-tuple-element.23, f32[2,4096]{1,0:T(2,128)S(1)} %get-tuple-element.22), channel_id=1, replica_groups=mesh['seq'=8,'expert'=32] {'seq'}, use_global_device_ids=true, to_apply=%region_7.0 | all-reduce | flops 16384 | bytes 98304 | tf_op jit(solution)/shard_map/psum | solution.py:28
  512.3 2.0 fusion.7
  514.3 0.0 copy-done
  514.3 0.4 convolution_bitcast_fusion.1
  514.7 0.7 fusion.40
  515.4 0.5 copy-done.2
  515.9 0.6 convolution_bitcast_fusion
  516.5 33.2 %all-reduce.4 = (bf16[1,2,4096]{2,1,0:T(2,128)(2,1)S(1)}, bf16[1,2,4096]{2,1,0:T(2,128)(2,1)S(1)}) all-reduce(f32[1,2,4096]{2,1,0:T(2,128)S(1)} %convolution_bitcast_fusion.1, f32[1,2,4096]{2,1,0:T(2,128)S(1)} %convolution_bitcast_fusion), channel_id=1, replica_groups=mesh['seq'=8,'expert'=32] {'seq'}, use_global_device_ids=true, to_apply=%region_8.0 | all-reduce | flops 16384 | bytes 98304 | tf_op jit(solution)/shard_map/psum | solution.py:41
  549.8 40.3 %all-gather.1 = bf16[1,64,4096]{2,0,1:T(2,128)(2,1)S(1)} all-gather(bf16[1,2,4096]{2,0,1:T(2,128)(2,1)S(1)} %copy.13), channel_id=3, replica_groups=mesh['seq'=8,'expert'=32] {'expert'}, dimensions={1}, use_global_device_ids=true | all-gather | bytes 540672 | tf_op jit(solution)/shard_map/all_gather | solution.py:75
  590.1 1.0 copy-done.5
  591.1 0.9 fusion.20
  592.0 77.0 %psum.54 = f32[64]{0:T(128)S(1)} all-reduce(f32[64]{0:T(128)S(1)} %get-tuple-element.20), channel_id=1, replica_groups=mesh['seq'=8,'expert'=32] {'seq','expert'}, use_global_device_ids=true, to_apply=%region_13.0 | all-reduce | flops 64 | bytes 512 | tf_op jit(solution)/shard_map/psum | solution.py:81
  669.0 43.0 %all-gather = bf16[1,64,4096]{2,0,1:T(2,128)(2,1)S(1)} all-gather(bf16[1,2,4096]{2,0,1:T(2,128)(2,1)S(1)} %copy.12), channel_id=2, replica_groups=mesh['seq'=8,'expert'=32] {'expert'}, dimensions={1}, use_global_device_ids=true | all-gather | bytes 540672 | tf_op jit(solution)/shard_map/all_gather | solution.py:43
  711.9 1.0 copy-done.7
  712.9 2.0 fusion.23
  714.9 0.1 fusion.22
  715.0 1.3 fusion.48
  716.4 0.0 all-reduce.9.cloned.1.call-update
  716.4 0.0 copy-start.8
  716.4 2.1 fusion
  718.5 2.1 fusion.1
  720.6 1.8 convolution_convert_fusion.2
  722.4 0.9 fusion.11
  723.3 0.0 copy-done.3
  723.3 1.4 fusion.2
  724.7 258.2 %all-reduce.9.cloned.1.call-done = f32[64,4096]{1,0:T(8,128)} async-done(((f32[64,4096]{1,0:T(8,128)}), f32[64,4096]{1,0:T(8,128)}) %all-reduce.9.cloned.1.call-update) | async-done | bytes 1048592
  982.9 0.9 constant_dynamic-slice_fusion
  983.8 30.2 %psum.55 = f32[2,4096]{1,0:T(2,128)} all-reduce(f32[2,4096]{1,0:T(2,128)S(1)} %constant_dynamic-slice_fusion), channel_id=1, replica_groups=mesh['seq'=8,'expert'=32] {'seq'}, use_global_device_ids=true, to_apply=%region_16.0 | all-reduce | flops 8192 | bytes 65536 | tf_op jit(solution)/shard_map/psum | solution.py:90
  (11 shorter events, 0.1 us)
Async XLA Ops:
  7.2 507.1 %copy-start = (bf16[1,256,4096]{2,1,0:T(8,128)(2,1)S(1)}, bf16[1,256,4096]{2,1,0:T(8,128)(2,1)}, u32[]{:S(2)}) copy-start(bf16[1,256,4096]{2,1,0:T(8,128)(2,1)} %param.8) | copy-start | bytes 6291460
  7.2 201.9 %copy-start.1 = (bf16[128,4096]{1,0:T(8,128)(2,1)S(1)}, bf16[128,4096]{1,0:T(8,128)(2,1)}, u32[]{:S(2)}) copy-start(bf16[128,4096]{1,0:T(8,128)(2,1)} %param.5) | copy-start | bytes 3145732
  7.2 474.3 %all-reduce.11.cloned.1.call-start = ((), (), s32[]{:S(2)}) async-start(), calls=%async_computation.1 | async-start | bytes 4194304
  209.0 1.4 copy-start.4
  210.3 1.3 copy-start.9
  211.6 771.3 %all-reduce.9.cloned.1.call-start = ((), (), s32[]{:S(2)}) async-start(), calls=%async_computation | async-start | bytes 2097152
  514.3 1.6 copy-start.2
  590.1 1.0 copy-start.5
  711.9 1.0 copy-start.7
  716.4 4.2 copy-start.8
  718.5 3.9 copy-start.6
  720.6 2.7 copy-start.3
Sparse Core Ops, SparseCore 0:
  211.8 269.6 all-reduce.10
  716.5 266.3 all-reduce.8
where the time goes:
time: 1030 us; the launch traced here: 1020 us
  waiting for transfers between devices  527 us (51%)
  blocking collectives  451 us (44%)
  matrix products  20.7 us (2%)
  between operations  14.8 us (1%)
    unnamed x4, waiting for transfers between devices  527 us
    psum x1, blocking collectives, body(): lax.psum(jnp.sum(dispatch_wide * pick_grad, axis=1), ('seq', 'expert'))  77 us
    psum x1, blocking collectives, body(): totals = lax.psum(jnp.sum(row_exp, axis=1), ('seq', 'expert'))  74.3 us
    pmax x1, blocking collectives, body(): peak_max = lax.pmax(local_peak, ('seq', 'expert'))  73.9 us
    psum x2, blocking collectives, body(): lax.psum(lax.psum_scatter(jnp.dot(weights, tokens, preferred_element_type...  60.1 us
    all_gather x1, blocking collectives, body(): keys_all = lax.all_gather(slot_keys, 'expert', axis=0, tiled=True)  49.3 us
    all_gather x1, blocking collectives, body(): portion = lax.all_gather(out_rows, 'expert', axis=0, tiled=True)  43 us
    all_gather x1, blocking collectives, body(): portion = lax.all_gather(slot_grad, 'expert', axis=0, tiled=True)  40.3 us
  transfers between devices with their start and end apart: 2, of which 2 were waited for; matrix products, arithmetic and copies ran while one was open for 1% of the time, Pallas kernels for 0%

commit v1 on v0

v1 whole, which is shorter than its diff:
```python
import jax
import jax.numpy as jnp
from jax import lax
from jax.sharding import PartitionSpec as P

F32 = jnp.float32
BF16 = jnp.bfloat16


def gelu_tanh(values):
    return jax.nn.gelu(values, approximate=True)


def split_f32(values):
    high = lax.reduce_precision(values, 8, 7)
    rest = values - high
    middle = lax.reduce_precision(rest, 8, 7)
    return [high.astype(BF16), middle.astype(BF16), (rest - middle).astype(BF16)]


def with_stats(values, stats):
    pieces = [p[..., None] for s in stats for p in split_f32(s)]
    lead = values.shape[:-1]
    pad = jnp.zeros(lead + (128 - len(pieces),), BF16)
    return jnp.concatenate([values.astype(BF16)] + pieces + [pad], axis=-1)


def read_stats(message, width, count):
    cols = message[..., width : width + 3 * count].astype(F32)
    return [cols[..., 3 * i] + cols[..., 3 * i + 1] + cols[..., 3 * i + 2] for i in range(count)]


def body(tokens, slot_keys, w_in, w_out, cotangent):
    width = tokens.shape[1]
    seq = lax.axis_size("seq")
    experts = lax.axis_size("expert")
    half = experts // 2
    same_core = [[2 * i + c for i in range(half)] for c in range(2)]
    partner = [(i, i ^ 1) for i in range(experts)]

    def swap(values):
        return lax.ppermute(values, "expert", partner)

    def exchange(values):
        return lax.all_to_all(values, "expert", 0, 0, tiled=True, axis_index_groups=same_core)

    def gather_half(values):
        return exchange(jnp.broadcast_to(values[None], (half,) + values.shape))

    def gather_seq(values):
        return lax.all_to_all(
            jnp.broadcast_to(values[None], (seq,) + values.shape), "seq", 0, 0, tiled=True
        )

    rows = slot_keys.shape[0]
    own = half * rows
    keys_own = gather_half(slot_keys).reshape(own, width)
    keys_all = jnp.concatenate([keys_own, swap(keys_own)], axis=0)

    logits = jnp.einsum("jd,td->jt", keys_all, tokens, preferred_element_type=F32)
    col_peak = jnp.max(logits, axis=0, keepdims=True)
    col_exp = jnp.exp(logits - col_peak)
    combine = (col_exp / jnp.sum(col_exp, axis=0, keepdims=True)).astype(BF16)
    combine_wide = combine.astype(F32)
    peak = jnp.max(logits, axis=1)
    row_exp = jnp.exp(logits - peak[:, None])
    total = jnp.sum(row_exp, axis=1)
    part_in = jnp.dot(row_exp.astype(BF16), tokens, preferred_element_type=F32)
    part_grad = jnp.dot(combine, cotangent, preferred_element_type=F32)

    def merge(first, second, peaks, totals):
        top = jnp.max(peaks, axis=0)
        scale = jnp.exp(peaks - top)
        return (
            jnp.sum(first.astype(F32) * scale[..., None], axis=0),
            jnp.sum(second.astype(F32), axis=0),
            top,
            jnp.sum(totals * scale, axis=0),
        )

    def merge_messages(message):
        peaks, totals = read_stats(message, 2 * width, 2)
        return merge(message[..., :width], message[..., width : 2 * width], peaks, totals)

    def pack(first, second, peaks, totals):
        return with_stats(jnp.concatenate([first, second], axis=-1), [peaks, totals])

    other = swap(pack(part_in[own:], part_grad[own:], peak[own:], total[own:]))
    other_peak, other_total = read_stats(other, 2 * width, 2)
    merged = merge(
        jnp.stack([part_in[:own], other[:, :width].astype(F32)]),
        jnp.stack([part_grad[:own], other[:, width : 2 * width].astype(F32)]),
        jnp.stack([peak[:own], other_peak]),
        jnp.stack([total[:own], other_total]),
    )
    message = exchange(pack(*merged).reshape(half, rows, -1))
    message = gather_seq(pack(*merge_messages(message)))
    slot_sum, out_sum, slot_peak, slot_total = merge_messages(message)
    slot_sum = slot_sum / slot_total[:, None]
    slot_in = slot_sum.astype(BF16)
    out_grad = out_sum.astype(BF16)

    w_first, w_second = w_in[0], w_out[0]
    pre_act = jnp.dot(slot_in, w_first, preferred_element_type=F32)
    hidden_act = gelu_tanh(pre_act).astype(BF16)
    out_part = jnp.dot(hidden_act, w_second, preferred_element_type=F32)
    act_grad = jnp.einsum("sd,fd->sf", out_grad, w_second, preferred_element_type=F32)
    _, pullback = jax.vjp(gelu_tanh, pre_act)
    pre_grad = pullback(act_grad)[0].astype(BF16)
    slot_part = jnp.einsum("sf,df->sd", pre_grad, w_first, preferred_element_type=F32)
    w_out_grad = jnp.einsum(
        "sf,sd->fd", hidden_act, out_grad, preferred_element_type=F32
    ).astype(BF16)[None]
    w_in_grad = jnp.einsum(
        "sd,sf->df", slot_in, pre_grad, preferred_element_type=F32
    ).astype(BF16)[None]

    parts = jnp.concatenate([out_part, slot_part], axis=0).astype(BF16)
    sums = jnp.sum(gather_seq(parts).astype(F32), axis=0).astype(BF16)
    crossing_own = jnp.sum(sums[rows:].astype(F32) * slot_sum, axis=1)
    message = with_stats(
        sums,
        [
            jnp.concatenate([slot_peak, crossing_own]),
            jnp.concatenate([slot_total, jnp.zeros_like(crossing_own)]),
        ],
    )
    message = gather_half(message)
    message = jnp.concatenate([message, swap(message)], axis=0)
    stat_one, stat_two = read_stats(message, width, 2)
    slot_out = message[:, :rows, :width].reshape(2 * own, width)
    slot_grad = message[:, rows:, :width].reshape(2 * own, width)
    peak_all = stat_one[:, :rows].reshape(2 * own, 1)
    crossing = stat_one[:, rows:].reshape(2 * own, 1)
    total_all = stat_two[:, :rows].reshape(2 * own, 1)

    dispatch = (jnp.exp(logits - peak_all) / total_all).astype(BF16)
    layer_out = jnp.einsum("jt,jd->td", combine, slot_out, preferred_element_type=F32).astype(BF16)
    combine_dot = jnp.einsum("jd,td->jt", slot_out, cotangent, preferred_element_type=F32)
    combine_grad = combine_wide * (
        combine_dot - jnp.sum(combine_wide * combine_dot, axis=0, keepdims=True)
    )
    pick_grad = jnp.einsum("jd,td->jt", slot_grad, tokens, preferred_element_type=F32)
    logit_grad = (dispatch.astype(F32) * (pick_grad - crossing) + combine_grad).astype(BF16)
    key_part = jnp.dot(logit_grad, tokens, preferred_element_type=F32)
    token_grad = jnp.einsum(
        "jt,jd->td",
        jnp.concatenate([dispatch, logit_grad], axis=0),
        jnp.concatenate([slot_grad, keys_all], axis=0),
        preferred_element_type=F32,
    ).astype(BF16)

    key_sum = key_part[:own] + swap(key_part[own:].astype(BF16)).astype(F32)
    key_sum = exchange(key_sum.astype(BF16).reshape(half, rows, width))
    key_sum = jnp.sum(key_sum.astype(F32), axis=0)
    key_grad = jnp.sum(gather_seq(key_sum), axis=0)
    return (layer_out, token_grad, key_grad, w_in_grad, w_out_grad)


def solution(mesh):
    in_specs = (
        P(("seq", "expert"), None),
        P("expert", None),
        P("expert", None, "seq"),
        P("expert", "seq", None),
        P(("seq", "expert"), None),
    )
    out_specs = (
        P(("seq", "expert"), None),
        P(("seq", "expert"), None),
        P("expert", None),
        P("expert", None, "seq"),
        P("expert", "seq", None),
    )
    return jax.shard_map(body, mesh=mesh, in_specs=in_specs, out_specs=out_specs, check_vma=False)
```

time: 1030 us -> 189 us (0.18)
  waiting for transfers between devices: 527 us -> 24.5 us
  blocking collectives: 451 us -> 79.9 us
  local copies, waits for them, and re-layouts: 7.1 us -> 34.8 us
  between operations: 14.8 us -> 0.91 us
  other arithmetic: 0.36 us -> 14.2 us
  starting transfers between devices: 0.08 us -> 13.1 us
    unnamed x4 -> x0, waiting for transfers between devices: 527 us -> none
    psum x5 -> x0, blocking collectives: 245 us -> none  [the longest x1 77 us: body(): lax.psum(jnp.sum(dispatch_wide * pick_grad, axis=1), ('seq', 'expert'))]
    all_gather x3 -> x0, blocking collectives: 133 us -> none  [the longest x1 49.3 us: body(): keys_all = lax.all_gather(slot_keys, 'expert', axis=0, tiled=True)]
    all_to_all x0 -> x4, blocking collectives: none -> 79.9 us  [the longest x3 69 us: exchange(): lax.all_to_all(values, 'expert', 0, 0, tiled=True, axis_index_groups=same...]
    pmax x1 -> x0, blocking collectives: 73.9 us -> none  [body(): peak_max = lax.pmax(local_peak, ('seq', 'expert'))]
    all_to_all x0 -> x3, waiting for transfers between devices: none -> 19.5 us  [the longest x2 10.5 us: gather_seq(): lax.all_to_all(jnp.broadcast_to(values[None], (seq,) + values.shape), 'se...]
    all_to_all x0 -> x3, starting transfers between devices: none -> 12.8 us  [the longest x2 9.25 us: gather_seq(): lax.all_to_all(jnp.broadcast_to(values[None], (seq,) + values.shape), 'se...]
    dot_general x15 -> x14, matrix products: 20.7 us -> 19.9 us  [the longest x1 2.73 us: body(): pre_act = jnp.dot(slot_in, w_first, preferred_element_type=F32)]
  transfers between devices with their start and end apart: 2 -> 7, of which waited for: 2 -> 7; matrix products, arithmetic and copies ran while one was open for 1% -> 5% of each run, Pallas kernels for 0% -> 0%
where the time goes in v1:
time: 189 us; the launch traced here: 187 us
  blocking collectives  79.9 us (42%)
  local copies, waits for them, and re-layouts  34.8 us (18%)
  waiting for transfers between devices  24.5 us (13%)
  matrix products  19.9 us (11%)
  other arithmetic  14.2 us (8%)
  starting transfers between devices  13.1 us (7%)
    all_to_all x3, blocking collectives, exchange(): lax.all_to_all(values, 'expert', 0, 0, tiled=True, axis_index_groups=same...  69 us
    all_to_all x1, blocking collectives, gather_seq(): lax.all_to_all(jnp.broadcast_to(values[None], (seq,) + values.shape), 'se...  10.9 us
    all_to_all x2, waiting for transfers between devices, gather_seq(): lax.all_to_all(jnp.broadcast_to(values[None], (seq,) + values.shape), 'se...  10.5 us
    all_to_all x2, starting transfers between devices, gather_seq(): lax.all_to_all(jnp.broadcast_to(values[None], (seq,) + values.shape), 'se...  9.25 us
    all_to_all x1, waiting for transfers between devices, exchange(): lax.all_to_all(values, 'expert', 0, 0, tiled=True, axis_index_groups=same...  8.95 us
    concatenate x5, local copies, waits for them, and re-layouts, with_stats(): return jnp.concatenate([values.astype(BF16)] + pieces + [pad], axis=-1)  6.26 us
    unnamed x28, local copies, waits for them, and re-layouts  5.5 us
    ppermute x4, waiting for transfers between devices, swap(): return lax.ppermute(values, 'expert', partner)  5.02 us
  transfers between devices with their start and end apart: 7, of which 7 were waited for; matrix products, arithmetic and copies ran while one was open for 5% of the time, Pallas kernels for 0%

profile of v1, /device:TPU:2, one launch (start us, length us, event | category | flops | bytes accessed | tf_op | source)
XLA Modules:
  0.0 187.3 jit_solution(2745697388737512188)
XLA Ops:
  0.7 1.1 broadcast_in_dim.36
  1.7 24.5 %all_to_all.35 = bf16[16,2,4096]{2,1,0:T(2,128)(2,1)S(1)} all-to-all(bf16[16,2,4096]{2,1,0:T(2,128)(2,1)S(1)} %broadcast_in_dim.36), channel_id=1, replica_groups={{0,2,4,6,8,10,12,14,16,18,20,22,24,26,28,30},{1,3,5,7,9,11,13,15,17,19,..., dimensions={0} | all-to-all | bytes 524288 | tf_op jit(solution)/shard_map/all_to_all | solution.py:45
  26.3 0.8 reshape.408
  27.1 1.7 collective-permute-done
  28.8 2.0 %fusion.78 = (f32[64]{0:T(128)S(1)}, f32[128]{0:T(128)S(1)}, f32[64,128]{1,0:T(8,128)S(1)}) fusion(bf16[128,4096]{1,0:T(8,128)(2,1)} %param.5, bf16[32,4096]{1,0:T(8,128)(2,1)S(1)} %collective-permute-done, bf16[32,4096]{1,0:T(8,128)(2,1)} %reshape.408), kind=kOutput, calls=%fused_computation.167 | convolution fusion | flops 68173632 | bytes 1606400 | tf_op jit(solution)/shard_map/jd,td->jt/dot_general | solution.py:60
  30.9 1.3 fusion.33
  33.2 1.5 fusion.84
  34.7 1.0 copy-done.4
  35.7 1.8 slice.338
  37.5 1.8 concatenate.95
  39.4 1.9 slice_bitcast_fusion
  41.4 0.8 copy-done.8
  42.2 1.8 fusion.19
  44.0 1.1 concatenate.97
  46.2 1.0 fusion.24
  47.2 2.0 %fusion.11 = bf16[32,4096]{1,0:T(8,128)(2,1)} fusion(f32[1,32,4096]{2,1,0:T(8,128)S(1)} %fusion.24, f32[1,32,4096]{2,1,0:T(8,128)} %slice_bitcast_fusion, f32[2,32]{1,0:T(2,128)S(1)} %get-tuple-element.16), kind=kLoop, calls=%fused_computation.20 | loop fusion | flops 655360 | bytes 1310976 | tf_op jit(solution)/shard_map/reduce_sum | solution.py:75
  49.1 1.8 concatenate.96
  51.5 4.3 %concatenate.102 = bf16[16,2,8320]{2,1,0:T(2,128)(2,1)} concatenate(bf16[16,2,4096]{2,1,0:T(2,128)(2,1)} %concatenate.96, bf16[16,2,4096]{2,1,0:T(2,128)(2,1)S(1)} %concatenate.97, bf16[16,2,1]{2,1,0:T(2,128)(2,1)S(1)} %bitcast.118, bf16[16,2,1]{2,1,0:T(2,128)(2,1)S(1)} %bitcast.117, bf16[16,2,1]{2,1,0:T(2,128)(2,1)S(1)} %bitcast.116, bf16[16,2,1]{2,1,0:T(2,128)(2,1)S(1)} %copy.347, ...), dimensions={2} | concatenate | bytes 1064960 | tf_op jit(solution)/shard_map/concatenate | solution.py:25
  55.8 24.1 %all_to_all.36 = bf16[16,2,8320]{2,1,0:T(2,128)(2,1)S(1)} all-to-all(bf16[16,2,8320]{2,1,0:T(2,128)(2,1)} %concatenate.102), channel_id=1, replica_groups={{0,2,4,6,8,10,12,14,16,18,20,22,24,26,28,30},{1,3,5,7,9,11,13,15,17,19,..., dimensions={0} | all-to-all | bytes 1064960 | tf_op jit(solution)/shard_map/all_to_all | solution.py:45
  79.9 0.8 copy-done.5
  81.9 1.2 slice_reduce_fusion
  83.1 1.3 multiply_reduce_fusion.1
  84.7 10.9 %all_to_all.37 = bf16[8,2,8320]{2,1,0:T(2,128)(2,1)S(1)} all-to-all(bf16[8,2,8320]{2,1,0:T(2,128)(2,1)S(1)} %broadcast_in_dim.44), channel_id=1, replica_groups=mesh['seq'=8,'expert'=32] {'seq'}, dimensions={0} | all-to-all | bytes 532480 | tf_op jit(solution)/shard_map/all_to_all | solution.py:51
  96.5 2.0 %copy.376 = f32[2,4096]{0,1:T(8,128)} copy(f32[2,4096]{1,0:T(2,128)S(1)} %multiply_reduce_fusion.2) | data formatting | bytes 65536
  98.5 2.7 %fusion.6 = f32[2,256]{1,0:T(2,128)S(1)} fusion(bf16[1,4096,256]{2,1,0:T(8,128)(2,1)} %param.7, f32[2,4096]{0,1:T(8,128)} %copy.376, f32[2]{0:T(128)S(1)} %fusion.51), kind=kOutput, calls=%fused_computation.12 | convolution fusion | flops 4210688 | bytes 2131976 | tf_op jit(solution)/shard_map/dot_general | solution.py:104
  103.5 0.8 broadcast_in_dim.45
  104.3 4.7 %all-to-all-start.3 = ((bf16[8,4,4096]{2,1,0:T(4,128)(2,1)}), bf16[8,4,4096]{2,1,0:T(4,128)(2,1)S(1)}, u32[]{:S(2)}, u32[]{:S(2)}) async-start(bf16[8,4,4096]{2,1,0:T(4,128)(2,1)} %broadcast_in_dim.45), calls=%async_computation.3 | async-start | bytes 524288 | tf_op jit(solution)/shard_map/all_to_all | solution.py:51
  109.3 5.8 %all-to-all-done.3 = bf16[8,4,4096]{2,1,0:T(4,128)(2,1)S(1)} async-done(((bf16[8,4,4096]{2,1,0:T(4,128)(2,1)}), bf16[8,4,4096]{2,1,0:T(4,128)(2,1)S(1)}, u32[]{:S(2)}, u32[]{:S(2)}) %all-to-all-start.3) | async-done | bytes 262176 | tf_op jit(solution)/shard_map/all_to_all | solution.py:51
  115.3 2.0 %copy.363 = f32[2,4096]{0,1:T(8,128)} copy(f32[2,4096]{1,0:T(2,128)S(1)} %slice_convert_fusion.4) | data formatting | bytes 65536 | tf_op jit(solution)/shard_map/convert_element_type | solution.py:120
  117.3 2.8 %multiply_reduce_fusion = f32[2]{0:T(128)S(1)} fusion(f32[2,4096]{0,1:T(8,128)} %copy.363, f32[2,4096]{0,1:T(8,128)} %copy.376, f32[2]{0:T(128)S(1)} %fusion.51), kind=kLoop, calls=%fused_computation.14 | loop fusion | flops 24574 | bytes 65552 | tf_op jit(solution)/shard_map/reduce_sum | solution.py:120
  120.7 20.3 %all_to_all.38 = bf16[16,4,4224]{2,1,0:T(4,128)(2,1)S(1)} all-to-all(bf16[16,4,4224]{2,1,0:T(4,128)(2,1)S(1)} %broadcast_in_dim.50), channel_id=1, replica_groups={{0,2,4,6,8,10,12,14,16,18,20,22,24,26,28,30},{1,3,5,7,9,11,13,15,17,19,..., dimensions={0} | all-to-all | bytes 1081344 | tf_op jit(solution)/shard_map/all_to_all | solution.py:45
  141.2 1.7 collective-permute-done.2
  143.2 2.1 %fusion.82 = (bf16[32,2,4096]{2,1,0:T(2,128)(2,1)}, bf16[32,2,4096]{2,1,0:T(2,128)(2,1)}) fusion(bf16[32,4,4224]{2,1,0:T(4,128)(2,1)S(1)} %constant_dynamic-update-slice_fusion), kind=kLoop, calls=%fused_computation.170 | loop fusion | bytes 2097152 | tf_op jit(solution)/shard_map/slice | solution.py:132
  145.3 2.0 %reshape.410 = bf16[64,4096]{1,0:T(8,128)(2,1)} reshape(bf16[32,2,4096]{2,1,0:T(2,128)(2,1)} %get-tuple-element.19) | data formatting | bytes 1048576 | tf_op jit(solution)/shard_map/reshape | solution.py:132
  148.4 2.0 %reshape.409 = bf16[64,4096]{1,0:T(8,128)(2,1)} reshape(bf16[32,2,4096]{2,1,0:T(2,128)(2,1)} %get-tuple-element.20) | data formatting | bytes 1048576 | tf_op jit(solution)/shard_map/reshape | solution.py:131
  150.4 1.9 %fusion.25 = (f32[128]{0:T(128)S(1)}, f32[64,128]{1,0:T(8,128)S(1)}) fusion(bf16[64,128]{1,0:T(8,128)(2,1)S(1)} %divide_convert_fusion.1, bf16[64,4096]{1,0:T(8,128)(2,1)} %reshape.409, bf16[128,4096]{1,0:T(8,128)(2,1)} %param.9), kind=kOutput, calls=%fused_computation.53 | convolution fusion | flops 67133312 | bytes 1622528 | tf_op jit(solution)/shard_map/jd,td->jt/dot_general | solution.py:139
  152.4 1.5 fusion.10
  154.5 1.4 collective-permute-done.3
  156.0 0.9 reshape.411
  156.9 3.5 %all-to-all-start.5 = ((bf16[16,2,4096]{2,1,0:T(2,128)(2,1)}), bf16[16,2,4096]{2,1,0:T(2,128)(2,1)S(1)}, u32[]{:S(2)}, u32[]{:S(2)}) async-start(bf16[16,2,4096]{2,1,0:T(2,128)(2,1)} %reshape.411), calls=%async_computation.5 | async-start | bytes 524288 | tf_op jit(solution)/shard_map/all_to_all | solution.py:45
  160.4 2.1 %fusion.1 = bf16[1,256,4096]{2,1,0:T(8,128)(2,1)} fusion(bf16[2,4096]{1,0:T(2,128)(2,1)S(1)} %get-tuple-element.21, f32[2,256]{1,0:T(2,128)S(1)} %fusion.6), kind=kOutput, calls=%fused_computation.3 | convolution fusion | flops 5247488 | bytes 2115584 | tf_op jit(solution)/shard_map/sf,sd->fd/dot_general | solution.py:111
  162.5 2.0 %fusion = bf16[1,4096,256]{2,1,0:T(8,128)(2,1)} fusion(bf16[2,256]{1,0:T(2,128)(2,1)S(1)} %fusion.45, f32[2,4096]{0,1:T(8,128)S(1)} %copy-done.2, f32[2]{0:T(128)S(1)} %fusion.51), kind=kOutput, calls=%fused_computation.2 | convolution fusion | flops 5259264 | bytes 2130952 | tf_op jit(solution)/shard_map/sd,sf->df/dot_general | solution.py:114
  164.5 1.4 convolution_convert_fusion.2
  166.0 9.0 %all-to-all-done.5 = bf16[16,2,4096]{2,1,0:T(2,128)(2,1)S(1)} async-done(((bf16[16,2,4096]{2,1,0:T(2,128)(2,1)}), bf16[16,2,4096]{2,1,0:T(2,128)(2,1)S(1)}, u32[]{:S(2)}, u32[]{:S(2)}) %all-to-all-start.5) | async-done | bytes 262176 | tf_op jit(solution)/shard_map/all_to_all | solution.py:45
  175.1 0.8 broadcast_in_dim.51
  175.9 4.6 %all-to-all-start.6 = ((f32[8,2,4096]{2,1,0:T(2,128)}), f32[8,2,4096]{2,1,0:T(2,128)S(1)}, u32[]{:S(2)}, u32[]{:S(2)}) async-start(f32[8,2,4096]{2,1,0:T(2,128)} %broadcast_in_dim.51), calls=%async_computation.6 | async-start | bytes 524288 | tf_op jit(solution)/shard_map/all_to_all | solution.py:51
  180.5 1.4 convolution_convert_fusion.3
  181.9 4.7 %all-to-all-done.6 = f32[8,2,4096]{2,1,0:T(2,128)S(1)} async-done(((f32[8,2,4096]{2,1,0:T(2,128)}), f32[8,2,4096]{2,1,0:T(2,128)S(1)}, u32[]{:S(2)}, u32[]{:S(2)}) %all-to-all-start.6) | async-done | bytes 262176 | tf_op jit(solution)/shard_map/all_to_all | solution.py:51
  (114 shorter events, 11.7 us)
Async XLA Ops:
  0.6 100.6 %copy-start = (bf16[1,256,4096]{2,1,0:T(8,128)(2,1)S(1)}, bf16[1,256,4096]{2,1,0:T(8,128)(2,1)}, u32[]{:S(2)}) copy-start(bf16[1,256,4096]{2,1,0:T(8,128)(2,1)} %param.8) | copy-start | bytes 6291460
  0.6 30.2 %copy-start.1 = (bf16[128,4096]{1,0:T(8,128)(2,1)S(1)}, bf16[128,4096]{1,0:T(8,128)(2,1)}, u32[]{:S(2)}) copy-start(bf16[128,4096]{1,0:T(8,128)(2,1)} %param.5) | copy-start | bytes 3145732
  27.1 1.7 collective-permute-start
  28.8 3.6 %copy-start.10 = (bf16[32,4096]{1,0:T(8,128)(2,1)}, bf16[32,4096]{1,0:T(8,128)(2,1)S(1)}, u32[]{:S(2)}) copy-start(bf16[32,4096]{1,0:T(8,128)(2,1)S(1)} %collective-permute-done) | copy-start | bytes 786436
  34.7 1.0 copy-start.4
  39.3 2.1 %collective-permute-start.1 = (bf16[32,8320]{1,0:T(8,128)(2,1)}, bf16[32,8320]{1,0:T(8,128)(2,1)S(1)}, u32[]{:S(2)}, u32[]{:S(2)}) collective-permute-start(bf16[32,8320]{1,0:T(8,128)(2,1)} %concatenate.95), channel_id=1, source_target_pairs={{0,1},{1,0},{2,3},{3,2},{4,5},{5,4},{6,7},{7,6},{8,9},{9,8},{10,11... | collective-permute-start | bytes 1597448 | tf_op jit(solution)/shard_map/ppermute | solution.py:42
  41.4 0.8 copy-start.8
  79.9 0.8 copy-start.5
  101.2 1.6 copy-start.6
  104.3 10.8 %all-to-all-start.3 = ((bf16[8,4,4096]{2,1,0:T(4,128)(2,1)}), bf16[8,4,4096]{2,1,0:T(4,128)(2,1)S(1)}, u32[]{:S(2)}, u32[]{:S(2)}) async-start(bf16[8,4,4096]{2,1,0:T(4,128)(2,1)} %broadcast_in_dim.45), calls=%async_computation.3 | async-start | bytes 524288 | tf_op jit(solution)/shard_map/all_to_all | solution.py:51
  141.0 1.9 %collective-permute-start.2 = (bf16[16,4,4224]{2,1,0:T(4,128)(2,1)S(1)}, bf16[16,4,4224]{2,1,0:T(4,128)(2,1)S(1)}, u32[]{:S(2)}, u32[]{:S(2)}) collective-permute-start(bf16[16,4,4224]{2,1,0:T(4,128)(2,1)S(1)} %all_to_all.38), channel_id=1, source_target_pairs={{0,1},{1,0},{2,3},{3,2},{4,5},{5,4},{6,7},{7,6},{8,9},{9,8},{10,11... | collective-permute-start | bytes 1622024 | tf_op jit(solution)/shard_map/ppermute | solution.py:42
  154.3 1.6 collective-permute-start.3
  156.9 18.1 %all-to-all-start.5 = ((bf16[16,2,4096]{2,1,0:T(2,128)(2,1)}), bf16[16,2,4096]{2,1,0:T(2,128)(2,1)S(1)}, u32[]{:S(2)}, u32[]{:S(2)}) async-start(bf16[16,2,4096]{2,1,0:T(2,128)(2,1)} %reshape.411), calls=%async_computation.5 | async-start | bytes 524288 | tf_op jit(solution)/shard_map/all_to_all | solution.py:45
  160.4 2.1 %copy-start.2 = (f32[2,4096]{0,1:T(8,128)S(1)}, f32[2,4096]{0,1:T(8,128)}, u32[]{:S(2)}) copy-start(f32[2,4096]{0,1:T(8,128)} %copy.376) | copy-start | bytes 98308
  162.5 2.0 %copy-start.7 = (bf16[64,4096]{1,0:T(8,128)(2,1)S(1)}, bf16[64,4096]{1,0:T(8,128)(2,1)}, u32[]{:S(2)}) copy-start(bf16[64,4096]{1,0:T(8,128)(2,1)} %reshape.410) | copy-start | bytes 1572868
  162.5 2.0 %copy-start.9 = (bf16[32,4096]{1,0:T(8,128)(2,1)S(1)}, bf16[32,4096]{1,0:T(8,128)(2,1)}, u32[]{:S(2)}) copy-start(bf16[32,4096]{1,0:T(8,128)(2,1)} %reshape.408) | copy-start | bytes 786436
  162.5 2.0 %copy-start.11 = (bf16[32,4096]{1,0:T(8,128)(2,1)S(1)}, bf16[32,4096]{1,0:T(8,128)(2,1)}, u32[]{:S(2)}) copy-start(bf16[32,4096]{1,0:T(8,128)(2,1)} %copy-done.10) | copy-start | bytes 786436
  164.5 16.0 %copy-start.3 = (bf16[64,4096]{1,0:T(8,128)(2,1)S(1)}, bf16[64,4096]{1,0:T(8,128)(2,1)}, u32[]{:S(2)}) copy-start(bf16[64,4096]{1,0:T(8,128)(2,1)} %reshape.409) | copy-start | bytes 1572868
  175.9 10.7 %all-to-all-start.6 = ((f32[8,2,4096]{2,1,0:T(2,128)}), f32[8,2,4096]{2,1,0:T(2,128)S(1)}, u32[]{:S(2)}, u32[]{:S(2)}) async-start(f32[8,2,4096]{2,1,0:T(2,128)} %broadcast_in_dim.51), calls=%async_computation.6 | async-start | bytes 524288 | tf_op jit(solution)/shard_map/all_to_all | solution.py:51

commit v2 on v0

v2 whole, which is shorter than its diff:
```python
import math

import jax
import jax.numpy as jnp
from jax import lax
from jax.experimental import pallas as pl
from jax.experimental.pallas import tpu as pltpu
from jax.sharding import PartitionSpec as P

F32 = jnp.float32
BF16 = jnp.bfloat16
LANES = 128
ROOT = math.sqrt(2.0 / math.pi)
CUBE = 0.044715


def dot(a, b, a_dim, b_dim):
    return lax.dot_general(a, b, (((a_dim,), (b_dim,)), ((), ())), preferred_element_type=F32)


def pieces(values):
    high = values.astype(BF16).astype(F32)
    rest = values - high
    middle = rest.astype(BF16).astype(F32)
    return [high, middle, rest - middle]


def stat_block(stats):
    lane = lax.broadcasted_iota(jnp.int32, (stats[0].shape[0], LANES), 1)
    block = jnp.zeros(lane.shape, F32)
    for i, piece in enumerate([p for s in stats for p in pieces(s)]):
        block = jnp.where(lane == i, piece, block)
    return block


def read_stat(block, i):
    cols = [block[..., k : k + 1].astype(F32) for k in range(3 * i, 3 * i + 3)]
    return cols[0] + cols[1] + cols[2]


def copies_kernel(values, out):
    for i in range(out.shape[0]):
        out[i] = values[...]


def dispatch_kernel(keys_own, keys_other, tokens, cotangent, keys_all, logits, combine, keep, send):
    width = tokens.shape[1]
    own = keep.shape[0]
    keys_all[:own] = keys_own[...].reshape(own, width)
    keys_all[own:] = keys_other[...].reshape(own, width)
    value = dot(keys_all[...], tokens[...], 1, 1)
    logits[...] = value
    col_exp = jnp.exp(value - jnp.max(value, axis=0, keepdims=True))
    weights = (col_exp / jnp.sum(col_exp, axis=0, keepdims=True)).astype(BF16)
    combine[...] = weights
    peak = jnp.max(value, axis=1, keepdims=True)
    row_exp = jnp.exp(value - peak)
    total = jnp.sum(row_exp, axis=1, keepdims=True)
    part = dot(row_exp.astype(BF16), tokens[...], 1, 0)
    keep[:, :width] = part[:own]
    send[:, :width] = part[own:].astype(BF16)
    part = dot(weights, cotangent[...], 1, 0)
    keep[:, width : 2 * width] = part[:own]
    send[:, width : 2 * width] = part[own:].astype(BF16)
    send[:, 2 * width :] = stat_block([peak[own:], total[own:]]).astype(BF16)
    lane = lax.broadcasted_iota(jnp.int32, (own, LANES), 1)
    keep[:, 2 * width :] = jnp.where(lane == 0, peak[:own], total[:own])


def pair_kernel(keep, other, out):
    width = (keep.shape[1] - LANES) // 2
    rows = keep.shape[0]
    stats = other[:, 2 * width :]
    peaks = [keep[:, 2 * width : 2 * width + 1], read_stat(stats, 0)]
    totals = [keep[:, 2 * width + 1 : 2 * width + 2], read_stat(stats, 1)]
    top = jnp.maximum(*peaks)
    scales = [jnp.exp(p - top) for p in peaks]
    first = keep[:, :width] * scales[0] + other[:, :width].astype(F32) * scales[1]
    out[:, :, :width] = first.astype(BF16).reshape(out.shape[0], out.shape[1], width)
    second = keep[:, width : 2 * width] + other[:, width : 2 * width].astype(F32)
    out[:, :, width : 2 * width] = second.astype(BF16).reshape(out.shape[0], out.shape[1], width)
    block = stat_block([top, totals[0] * scales[0] + totals[1] * scales[1]])
    out[:, :, 2 * width :] = block.astype(BF16).reshape(out.shape[0], out.shape[1], LANES)


def merge(message):
    width = (message.shape[2] - LANES) // 2
    stats = message[:, :, 2 * width :]
    peaks, totals = read_stat(stats, 0), read_stat(stats, 1)
    top = jnp.max(peaks, axis=0, keepdims=True)
    scales = jnp.exp(peaks - top)
    total = jnp.sum(totals * scales, axis=0)
    first = message[0, :, :width].astype(F32) * scales[0]
    for p in range(1, message.shape[0]):
        first += message[p, :, :width].astype(F32) * scales[p]
    second = message[0, :, width : 2 * width].astype(F32)
    for p in range(1, message.shape[0]):
        second += message[p, :, width : 2 * width].astype(F32)
    return first, second, top[0], total


def merge_kernel(message, out):
    width = (message.shape[2] - LANES) // 2
    first, second, top, total = merge(message)
    first, second = first.astype(BF16), second.astype(BF16)
    block = stat_block([top, total]).astype(BF16)
    for i in range(out.shape[0]):
        out[i, :, :width] = first
        out[i, :, width : 2 * width] = second
        out[i, :, 2 * width :] = block


def expert_kernel(
    message, w_in, w_out, parts, sums, stats, slot_in_out, out_grad_out, hidden_out, pre_grad_out
):
    width = sums.shape[1]
    first, second, top, total = merge(message)
    slot_sum = first / total
    sums[...] = slot_sum
    lane = lax.broadcasted_iota(jnp.int32, stats.shape, 1)
    stats[...] = jnp.where(lane == 0, top, total)
    slot_in = slot_sum.astype(BF16)
    out_grad = second.astype(BF16)
    slot_in_out[...] = slot_in
    out_grad_out[...] = out_grad
    pre_act = dot(slot_in, w_in[...], 1, 0)
    tanh = jnp.tanh(ROOT * (pre_act + CUBE * (pre_act * pre_act * pre_act)))
    hidden = (pre_act * (0.5 * (1.0 + tanh))).astype(BF16)
    hidden_out[...] = hidden
    act_grad = dot(out_grad, w_out[...], 1, 1)
    slope = 0.5 * (1.0 + tanh) + 0.5 * pre_act * (1.0 - tanh * tanh) * (
        ROOT * (1.0 + 3.0 * CUBE * (pre_act * pre_act))
    )
    pre_grad = (act_grad * slope).astype(BF16)
    pre_grad_out[...] = pre_grad
    out_part = dot(hidden, w_out[...], 1, 0).astype(BF16)
    slot_part = dot(pre_grad, w_in[...], 1, 1).astype(BF16)
    for i in range(parts.shape[0]):
        parts[i, :, :width] = out_part
        parts[i, :, width:] = slot_part


def outs_kernel(parts, sums, stats, out):
    width = sums.shape[1]
    total = parts[0].astype(F32)
    for p in range(1, parts.shape[0]):
        total += parts[p].astype(F32)
    values = total.astype(BF16)
    crossing = jnp.sum(values[:, width:].astype(F32) * sums[...], axis=1, keepdims=True)
    block = stat_block([stats[:, 0:1], stats[:, 1:2], crossing]).astype(BF16)
    for i in range(out.shape[0]):
        out[i, :, : 2 * width] = values
        out[i, :, 2 * width :] = block


def token_kernel(
    outs_own, outs_other, tokens, cotangent, logits, combine,
    slot_out, slot_grad, dispatch_out, logit_grad_out, keep, send,
):
    width = tokens.shape[1]
    own = keep.shape[0]
    blocks = []
    for i, outs in enumerate((outs_own, outs_other)):
        rows = pl.ds(i * own, own)
        slot_out[rows] = outs[:, :, :width].reshape(own, width)
        slot_grad[rows] = outs[:, :, width : 2 * width].reshape(own, width)
        blocks.append(outs[:, :, 2 * width :].reshape(own, LANES).astype(F32))
    block = jnp.concatenate(blocks, axis=0)
    peak, total, crossing = (read_stat(block, i) for i in range(3))
    dispatch = (jnp.exp(logits[...] - peak) / total).astype(BF16)
    dispatch_out[...] = dispatch
    weights = combine[...].astype(F32)
    combine_dot = dot(slot_out[...], cotangent[...], 1, 1)
    combine_grad = weights * (combine_dot - jnp.sum(weights * combine_dot, axis=0, keepdims=True))
    pick_grad = dot(slot_grad[...], tokens[...], 1, 1)
    logit_grad = (dispatch.astype(F32) * (pick_grad - crossing) + combine_grad).astype(BF16)
    logit_grad_out[...] = logit_grad
    part = dot(logit_grad, tokens[...], 1, 0)
    keep[...] = part[:own]
    send[...] = part[own:].astype(BF16)


def key_pair_kernel(keep, other, out):
    out[...] = (keep[...] + other[...].astype(F32)).astype(BF16).reshape(out.shape)


def key_merge_kernel(message, out):
    total = message[0].astype(F32)
    for p in range(1, message.shape[0]):
        total += message[p].astype(F32)
    for i in range(out.shape[0]):
        out[i] = total.astype(out.dtype)


def key_sum_kernel(message, out):
    total = message[0].astype(F32)
    for p in range(1, message.shape[0]):
        total += message[p].astype(F32)
    out[...] = total


def call(kernel, outs, *args):
    whole = pl.BlockSpec(memory_space=pltpu.VMEM)
    return pl.pallas_call(
        kernel,
        out_shape=[pltpu.VMEM(shape, dtype) for shape, dtype in outs],
        in_specs=[whole] * len(args),
        out_specs=[whole] * len(outs),
        compiler_params=pltpu.CompilerParams(vmem_limit_bytes=24 * 1024 * 1024),
    )(*args)


def body(tokens, slot_keys, w_in, w_out, cotangent):
    count, width = tokens.shape
    hidden_units = w_in.shape[2]
    seq = lax.axis_size("seq")
    experts = lax.axis_size("expert")
    rows = slot_keys.shape[0]
    half = experts // 2
    own = half * rows
    slots = 2 * own
    long = 2 * width + LANES
    same_core = [[2 * i + c for i in range(half)] for c in range(2)]
    partner = [(i, i ^ 1) for i in range(experts)]

    def swap(values):
        return lax.ppermute(values, "expert", partner)

    def exchange(values):
        return lax.all_to_all(values, "expert", 0, 0, tiled=True, axis_index_groups=same_core)

    def exchange_seq(values):
        return lax.all_to_all(values, "seq", 0, 0, tiled=True)

    (message,) = call(copies_kernel, [((half, rows, width), BF16)], slot_keys)
    keys_own = exchange(message)
    keys_all, logits, combine, keep, send = call(
        dispatch_kernel,
        [
            ((slots, width), BF16),
            ((slots, count), F32),
            ((slots, count), BF16),
            ((own, long), F32),
            ((own, long), BF16),
        ],
        keys_own, swap(keys_own), tokens, cotangent,
    )
    (message,) = call(pair_kernel, [((half, rows, long), BF16)], keep, swap(send))
    (message,) = call(merge_kernel, [((seq, rows, long), BF16)], exchange(message))
    parts, sums, stats, slot_in, out_grad, hidden, pre_grad = call(
        expert_kernel,
        [
            ((seq, rows, 2 * width), BF16),
            ((rows, width), F32),
            ((rows, LANES), F32),
            ((rows, width), BF16),
            ((rows, width), BF16),
            ((rows, hidden_units), BF16),
            ((rows, hidden_units), BF16),
        ],
        exchange_seq(message), w_in[0], w_out[0],
    )
    (message,) = call(
        outs_kernel, [((half, rows, long), BF16)], exchange_seq(parts), sums, stats
    )
    outs = exchange(message)
    slot_out, slot_grad, dispatch, logit_grad, keep, send = call(
        token_kernel,
        [
            ((slots, width), BF16),
            ((slots, width), BF16),
            ((slots, count), BF16),
            ((slots, count), BF16),
            ((own, width), F32),
            ((own, width), BF16),
        ],
        outs, swap(outs), tokens, cotangent, logits, combine,
    )
    (message,) = call(key_pair_kernel, [((half, rows, width), BF16)], keep, swap(send))
    (message,) = call(key_merge_kernel, [((seq, rows, width), F32)], exchange(message))
    (key_grad,) = call(key_sum_kernel, [((rows, width), F32)], exchange_seq(message))

    w_out_grad = dot(hidden, out_grad, 0, 0).astype(BF16)[None]
    w_in_grad = dot(slot_in, pre_grad, 0, 0).astype(BF16)[None]
    layer_out = dot(combine, slot_out, 0, 0).astype(BF16)
    token_grad = dot(
        jnp.concatenate([dispatch, logit_grad], axis=0),
        jnp.concatenate([slot_grad, keys_all], axis=0),
        0,
        0,
    ).astype(BF16)
    return (layer_out, token_grad, key_grad, w_in_grad, w_out_grad)


def solution(mesh):
    in_specs = (
        P(("seq", "expert"), None),
        P("expert", None),
        P("expert", None, "seq"),
        P("expert", "seq", None),
        P(("seq", "expert"), None),
    )
    out_specs = (
        P(("seq", "expert"), None),
        P(("seq", "expert"), None),
        P("expert", None),
        P("expert", None, "seq"),
        P("expert", "seq", None),
    )
    return jax.shard_map(body, mesh=mesh, in_specs=in_specs, out_specs=out_specs, check_vma=False)
```

time: 1030 us -> 137 us (0.13)
  waiting for transfers between devices: 527 us -> 20.3 us
  blocking collectives: 451 us -> 88.9 us
  between operations: 14.8 us -> 0.71 us
  matrix products: 20.7 us -> 7.01 us
    unnamed x4 -> x0, waiting for transfers between devices: 527 us -> none
    psum x5 -> x0, blocking collectives: 245 us -> none  [the longest x1 77 us: body(): lax.psum(jnp.sum(dispatch_wide * pick_grad, axis=1), ('seq', 'expert'))]
    all_gather x3 -> x0, blocking collectives: 133 us -> none  [the longest x1 49.3 us: body(): keys_all = lax.all_gather(slot_keys, 'expert', axis=0, tiled=True)]
    all_to_all x0 -> x5, blocking collectives: none -> 88.9 us  [the longest x3 67.9 us: exchange(): lax.all_to_all(values, 'expert', 0, 0, tiled=True, axis_index_groups=same...]
    pmax x1 -> x0, blocking collectives: 73.9 us -> none  [body(): peak_max = lax.pmax(local_peak, ('seq', 'expert'))]
    dot_general x15 -> x4, matrix products: 20.7 us -> 7.01 us  [dot(): lax.dot_general(a, b, (((a_dim,), (b_dim,)), ((), ())), preferred_element...]
    all_to_all x0 -> x2, waiting for transfers between devices: none -> 13.7 us  [the longest x1 8.94 us: exchange(): lax.all_to_all(values, 'expert', 0, 0, tiled=True, axis_index_groups=same...]
  transfers between devices with their start and end apart: 2 -> 6, of which waited for: 2 -> 6; matrix products, arithmetic and copies ran while one was open for 1% -> 5% of each run, Pallas kernels for 0% -> 0%
where the time goes in v2:
time: 137 us; the launch traced here: 136 us
  blocking collectives  88.9 us (65%)
  waiting for transfers between devices  20.3 us (15%)
  starting transfers between devices  8.55 us (6%)
  Pallas kernels  7.15 us (5%)
  matrix products  7.01 us (5%)
  local copies, waits for them, and re-layouts  3.81 us (3%)
    all_to_all x3, blocking collectives, exchange(): lax.all_to_all(values, 'expert', 0, 0, tiled=True, axis_index_groups=same...  67.9 us
    all_to_all x2, blocking collectives, exchange_seq(): return lax.all_to_all(values, 'seq', 0, 0, tiled=True)  21 us
    all_to_all x1, waiting for transfers between devices, exchange(): lax.all_to_all(values, 'expert', 0, 0, tiled=True, axis_index_groups=same...  8.94 us
    pallas_call x10, Pallas kernels, call(): pl.pallas_call(kernel, out_shape=[pltpu.VMEM(shape, dtype) for shape, dty...  7.15 us
    dot_general x4, matrix products, dot(): lax.dot_general(a, b, (((a_dim,), (b_dim,)), ((), ())), preferred_element...  7.01 us
    ppermute x4, waiting for transfers between devices, swap(): return lax.ppermute(values, 'expert', partner)  6.65 us
    all_to_all x1, waiting for transfers between devices, exchange_seq(): return lax.all_to_all(values, 'seq', 0, 0, tiled=True)  4.73 us
    all_to_all x1, starting transfers between devices, exchange_seq(): return lax.all_to_all(values, 'seq', 0, 0, tiled=True)  4.58 us
  transfers between devices with their start and end apart: 6, of which 6 were waited for; matrix products, arithmetic and copies ran while one was open for 5% of the time, Pallas kernels for 0%

profile of v2, /device:TPU:2, one launch (start us, length us, event | category | flops | bytes accessed | tf_op | source)
XLA Modules:
  0.0 136.4 jit_solution(5217177821066372452)
XLA Ops:
  0.6 0.0 copy-start.6
  0.6 0.7 copy-done.6
  1.4 24.5 %all_to_all.35.keys_own = bf16[16,2,4096]{2,1,0:T(2,128)(2,1)S(1)} all-to-all(bf16[16,2,4096]{2,1,0:T(2,128)(2,1)S(1)} %shard_map.92), channel_id=1, replica_groups={{0,2,4,6,8,10,12,14,16,18,20,22,24,26,28,30},{1,3,5,7,9,11,13,15,17,19,..., dimensions={0} | all-to-all | bytes 524288 | tf_op jit(solution)/shard_map/all_to_all | solution.py:230
  25.9 0.0 collective-permute-start
  25.9 1.5 %collective-permute-done.keys_other = bf16[16,2,4096]{2,1,0:T(2,128)(2,1)S(1)} collective-permute-done((bf16[16,2,4096]{2,1,0:T(2,128)(2,1)S(1)}, bf16[16,2,4096]{2,1,0:T(2,128)(2,1)S(1)}, u32[]{:S(2)}, u32[]{:S(2)}) %collective-permute-start) | collective-permute-done | bytes 262176 | tf_op jit(solution)/shard_map/ppermute | solution.py:227
  27.4 0.0 copy-start
  27.5 1.2 copy-done
  28.7 0.0 copy-start.2
  28.7 1.2 copy-done.2
  29.9 1.4 %shard_map.93 = (bf16[64,4096]{1,0:T(8,128)(2,1)S(1)}, f32[64,128]{1,0:T(8,128)S(1)}, bf16[64,128]{1,0:T(8,128)(2,1)S(1)}, f32[32,8320]{1,0:T(8,128)S(1)}, bf16[32,8320]{1,0:T(8,128)(2,1)S(1)}) custom-call(bf16[16,2,4096]{2,1,0:T(2,128)(2,1)S(1)} %all_to_all.35.keys_own, bf16[16,2,4096]{2,1,0:T(2,128)(2,1)S(1)} %collective-permute-done.keys_other, ...), custom_call_target="tpu_custom_call" | custom-call | tf_op jit(solution)/shard_map/pallas_call | solution.py:204
  31.3 0.2 collective-permute-start.1
  31.6 1.8 %collective-permute-done.1.other = bf16[32,8320]{1,0:T(8,128)(2,1)S(1)} collective-permute-done((bf16[32,8320]{1,0:T(8,128)(2,1)S(1)}, bf16[32,8320]{1,0:T(8,128)(2,1)S(1)}, u32[]{:S(2)}, u32[]{:S(2)}) %collective-permute-start.1) | collective-permute-done | bytes 532512 | tf_op jit(solution)/shard_map/ppermute | solution.py:227
  33.3 0.0 copy-start.4
  33.4 0.0 copy-start.5
  33.4 0.5 shard_map.94
  33.8 23.4 %all_to_all.36.message = bf16[16,2,8320]{2,1,0:T(2,128)(2,1)S(1)} all-to-all(bf16[16,2,8320]{2,1,0:T(2,128)(2,1)S(1)} %shard_map.94), channel_id=1, replica_groups={{0,2,4,6,8,10,12,14,16,18,20,22,24,26,28,30},{1,3,5,7,9,11,13,15,17,19,..., dimensions={0} | all-to-all | bytes 1064960 | tf_op jit(solution)/shard_map/all_to_all | solution.py:230
  57.2 0.3 shard_map.95
  57.5 10.9 %all_to_all.37.message = bf16[8,2,8320]{2,1,0:T(2,128)(2,1)S(1)} all-to-all(bf16[8,2,8320]{2,1,0:T(2,128)(2,1)S(1)} %shard_map.95), channel_id=1, replica_groups=mesh['seq'=8,'expert'=32] {'seq'}, dimensions={0} | all-to-all | bytes 532480 | tf_op jit(solution)/shard_map/all_to_all | solution.py:233
  68.4 0.0 copy-done.4
  68.4 0.0 copy-done.5
  68.4 2.0 %shard_map.96 = (bf16[8,2,8192]{2,1,0:T(2,128)(2,1)S(1)}, f32[2,4096]{1,0:T(2,128)S(1)}, f32[2,128]{1,0:T(2,128)S(1)}, bf16[2,4096]{1,0:T(2,128)(2,1)S(1)}, bf16...) custom-call(bf16[8,2,8320]{2,1,0:T(2,128)(2,1)S(1)} %all_to_all.37.message, ...), custom_call_target="tpu_custom_call" | custom-call | tf_op jit(solution)/shard_map/pallas_call | solution.py:204
  70.5 0.0 copy-start.1
  70.5 0.0 copy-start.3
  70.5 10.0 %all_to_all.38.parts = bf16[8,2,8192]{2,1,0:T(2,128)(2,1)S(1)} all-to-all(bf16[8,2,8192]{2,1,0:T(2,128)(2,1)S(1)} %get-tuple-element.26), channel_id=1, replica_groups=mesh['seq'=8,'expert'=32] {'seq'}, dimensions={0} | all-to-all | bytes 524288 | tf_op jit(solution)/shard_map/all_to_all | solution.py:233
  80.5 0.2 shard_map.97
  80.7 20.0 %all_to_all.39.outs_own = bf16[16,2,8320]{2,1,0:T(2,128)(2,1)S(1)} all-to-all(bf16[16,2,8320]{2,1,0:T(2,128)(2,1)S(1)} %shard_map.97), channel_id=1, replica_groups={{0,2,4,6,8,10,12,14,16,18,20,22,24,26,28,30},{1,3,5,7,9,11,13,15,17,19,..., dimensions={0} | all-to-all | bytes 1064960 | tf_op jit(solution)/shard_map/all_to_all | solution.py:230
  100.7 0.0 collective-permute-start.2
  100.7 1.9 %collective-permute-done.2.outs_other = bf16[16,2,8320]{2,1,0:T(2,128)(2,1)S(1)} collective-permute-done((bf16[16,2,8320]{2,1,0:T(2,128)(2,1)S(1)}, bf16[16,2,8320]{2,1,0:T(2,128)(2,1)S(1)}, u32[]{:S(2)}, u32[]{:S(2)}) %collective-permute-start.2) | collective-permute-done | bytes 532512 | tf_op jit(solution)/shard_map/ppermute | solution.py:227
  102.6 0.0 copy-done.1
  102.6 0.0 copy-done.3
  102.6 1.2 shard_map.98
  103.9 0.2 collective-permute-start.3
  104.1 1.4 %collective-permute-done.3.other = bf16[32,4096]{1,0:T(8,128)(2,1)S(1)} collective-permute-done((bf16[32,4096]{1,0:T(8,128)(2,1)S(1)}, bf16[32,4096]{1,0:T(8,128)(2,1)S(1)}, u32[]{:S(2)}, u32[]{:S(2)}) %collective-permute-start.3) | collective-permute-done | bytes 262176 | tf_op jit(solution)/shard_map/ppermute | solution.py:227
  105.5 0.8 shard_map.99
  106.3 3.5 %all-to-all-start.5 = ((bf16[16,2,4096]{2,1,0:T(2,128)(2,1)}), bf16[16,2,4096]{2,1,0:T(2,128)(2,1)S(1)}, u32[]{:S(2)}, u32[]{:S(2)}) async-start(bf16[16,2,4096]{2,1,0:T(2,128)(2,1)} %shard_map.99), calls=%async_computation.5 | async-start | bytes 524288 | tf_op jit(solution)/shard_map/all_to_all | solution.py:230
  109.8 2.1 %fusion = bf16[1,4096,256]{2,1,0:T(8,128)(2,1)} fusion(bf16[2,4096]{1,0:T(2,128)(2,1)S(1)} %get-tuple-element.37, bf16[2,256]{1,0:T(2,128)(2,1)S(1)} %get-tuple-element.38), kind=kOutput, calls=%fused_computation.2 | convolution fusion | flops 5242880 | bytes 2114560 | tf_op jit(solution)/shard_map/dot_general | solution.py:18
  111.9 2.1 %fusion.1 = bf16[1,256,4096]{2,1,0:T(8,128)(2,1)} fusion(bf16[2,256]{1,0:T(2,128)(2,1)S(1)} %get-tuple-element.39, bf16[2,4096]{1,0:T(2,128)(2,1)S(1)} %get-tuple-element.40), kind=kOutput, calls=%fused_computation.3 | convolution fusion | flops 5242880 | bytes 2114560 | tf_op jit(solution)/shard_map/dot_general | solution.py:18
  114.0 1.4 %convolution_convert_fusion.2 = bf16[128,4096]{1,0:T(8,128)(2,1)} fusion(bf16[64,4096]{1,0:T(8,128)(2,1)S(1)} %get-tuple-element.34, bf16[64,4096]{1,0:T(8,128)(2,1)S(1)} %get-tuple-element.33, bf16[64,128]{1,0:T(8,128)(2,1)S(1)} %get-tuple-element.32, bf16[64,128]{1,0:T(8,128)(2,1)S(1)} %get-tuple-element.31), kind=kOutput, calls=%fused_computation.4 | convolution fusion | flops 136904704 | bytes 2129920 | tf_op jit(solution)/shard_map/dot_general | solution.py:18
  115.4 8.9 %all-to-all-done.5.message = bf16[16,2,4096]{2,1,0:T(2,128)(2,1)S(1)} async-done(((bf16[16,2,4096]{2,1,0:T(2,128)(2,1)}), bf16[16,2,4096]{2,1,0:T(2,128)(2,1)S(1)}, u32[]{:S(2)}, u32[]{:S(2)}) %all-to-all-start.5) | async-done | bytes 262176 | tf_op jit(solution)/shard_map/all_to_all | solution.py:230
  124.3 0.7 shard_map.100
  125.1 4.6 %all-to-all-start.6 = ((f32[8,2,4096]{2,1,0:T(2,128)}), f32[8,2,4096]{2,1,0:T(2,128)S(1)}, u32[]{:S(2)}, u32[]{:S(2)}) async-start(f32[8,2,4096]{2,1,0:T(2,128)} %shard_map.100), calls=%async_computation.6 | async-start | bytes 524288 | tf_op jit(solution)/shard_map/all_to_all | solution.py:233
  129.6 1.4 %convolution_convert_fusion.3 = bf16[128,4096]{1,0:T(8,128)(2,1)} fusion(bf16[64,128]{1,0:T(8,128)(2,1)S(1)} %get-tuple-element.23.combine, bf16[64,4096]{1,0:T(8,128)(2,1)S(1)} %get-tuple-element.30), kind=kOutput, calls=%fused_computation.5 | convolution fusion | flops 67633152 | bytes 1589248 | tf_op jit(solution)/shard_map/dot_general | solution.py:18
  131.1 4.7 %all-to-all-done.6.message = f32[8,2,4096]{2,1,0:T(2,128)S(1)} async-done(((f32[8,2,4096]{2,1,0:T(2,128)}), f32[8,2,4096]{2,1,0:T(2,128)S(1)}, u32[]{:S(2)}, u32[]{:S(2)}) %all-to-all-start.6) | async-done | bytes 262176 | tf_op jit(solution)/shard_map/all_to_all | solution.py:233
  135.8 0.6 copy.10
  (2 shorter events, 0.0 us)
Async XLA Ops:
  0.6 0.7 copy-start.6
  25.9 1.5 %collective-permute-start = (bf16[16,2,4096]{2,1,0:T(2,128)(2,1)S(1)}, bf16[16,2,4096]{2,1,0:T(2,128)(2,1)S(1)}, u32[]{:S(2)}, u32[]{:S(2)}) collective-permute-start(bf16[16,2,4096]{2,1,0:T(2,128)(2,1)S(1)} %all_to_all.35.keys_own), channel_id=1, source_target_pairs={{0,1},{1,0},{2,3},{3,2},{4,5},{5,4},{6,7},{7,6},{8,9},{9,8},{10,11... | collective-permute-start | bytes 786440 | tf_op jit(solution)/shard_map/ppermute | solution.py:227
  27.4 1.2 copy-start
  28.7 1.2 copy-start.2
  31.3 2.0 %collective-permute-start.1 = (bf16[32,8320]{1,0:T(8,128)(2,1)S(1)}, bf16[32,8320]{1,0:T(8,128)(2,1)S(1)}, u32[]{:S(2)}, u32[]{:S(2)}) collective-permute-start(bf16[32,8320]{1,0:T(8,128)(2,1)S(1)} %get-tuple-element.25), channel_id=1, source_target_pairs={{0,1},{1,0},{2,3},{3,2},{4,5},{5,4},{6,7},{7,6},{8,9},{9,8},{10,11... | collective-permute-start | bytes 1597448 | tf_op jit(solution)/shard_map/ppermute | solution.py:227
  33.3 35.1 %copy-start.4 = (bf16[1,4096,256]{2,1,0:T(8,128)(2,1)S(1)}, bf16[1,4096,256]{2,1,0:T(8,128)(2,1)}, u32[]{:S(2)}) copy-start(bf16[1,4096,256]{2,1,0:T(8,128)(2,1)} %param.7) | copy-start | bytes 6291460
  33.4 35.1 %copy-start.5 = (bf16[1,256,4096]{2,1,0:T(8,128)(2,1)S(1)}, bf16[1,256,4096]{2,1,0:T(8,128)(2,1)}, u32[]{:S(2)}) copy-start(bf16[1,256,4096]{2,1,0:T(8,128)(2,1)} %param.8) | copy-start | bytes 6291460
  70.5 32.2 %copy-start.1 = (bf16[128,4096]{1,0:T(8,128)(2,1)S(1)}, bf16[128,4096]{1,0:T(8,128)(2,1)}, u32[]{:S(2)}) copy-start(bf16[128,4096]{1,0:T(8,128)(2,1)} %tokens.3) | copy-start | bytes 3145732
  70.5 32.2 %copy-start.3 = (bf16[128,4096]{1,0:T(8,128)(2,1)S(1)}, bf16[128,4096]{1,0:T(8,128)(2,1)}, u32[]{:S(2)}) copy-start(bf16[128,4096]{1,0:T(8,128)(2,1)} %cotangent.3) | copy-start | bytes 3145732
  100.7 1.9 %collective-permute-start.2 = (bf16[16,2,8320]{2,1,0:T(2,128)(2,1)S(1)}, bf16[16,2,8320]{2,1,0:T(2,128)(2,1)S(1)}, u32[]{:S(2)}, u32[]{:S(2)}) collective-permute-start(bf16[16,2,8320]{2,1,0:T(2,128)(2,1)S(1)} %all_to_all.39.outs_own), channel_id=1, source_target_pairs={{0,1},{1,0},{2,3},{3,2},{4,5},{5,4},{6,7},{7,6},{8,9},{9,8},{10,11... | collective-permute-start | bytes 1597448 | tf_op jit(solution)/shard_map/ppermute | solution.py:227
  103.9 1.6 %collective-permute-start.3 = (bf16[32,4096]{1,0:T(8,128)(2,1)S(1)}, bf16[32,4096]{1,0:T(8,128)(2,1)S(1)}, u32[]{:S(2)}, u32[]{:S(2)}) collective-permute-start(bf16[32,4096]{1,0:T(8,128)(2,1)S(1)} %get-tuple-element.36), channel_id=1, source_target_pairs={{0,1},{1,0},{2,3},{3,2},{4,5},{5,4},{6,7},{7,6},{8,9},{9,8},{10,11... | collective-permute-start | bytes 786440 | tf_op jit(solution)/shard_map/ppermute | solution.py:227
  106.3 18.1 %all-to-all-start.5 = ((bf16[16,2,4096]{2,1,0:T(2,128)(2,1)}), bf16[16,2,4096]{2,1,0:T(2,128)(2,1)S(1)}, u32[]{:S(2)}, u32[]{:S(2)}) async-start(bf16[16,2,4096]{2,1,0:T(2,128)(2,1)} %shard_map.99), calls=%async_computation.5 | async-start | bytes 524288 | tf_op jit(solution)/shard_map/all_to_all | solution.py:230
  125.1 10.7 %all-to-all-start.6 = ((f32[8,2,4096]{2,1,0:T(2,128)}), f32[8,2,4096]{2,1,0:T(2,128)S(1)}, u32[]{:S(2)}, u32[]{:S(2)}) async-start(f32[8,2,4096]{2,1,0:T(2,128)} %shard_map.100), calls=%async_computation.6 | async-start | bytes 524288 | tf_op jit(solution)/shard_map/all_to_all | solution.py:233

commit v3 on v2

v3 whole, which is shorter than its diff:
```python
import math

import jax
import jax.numpy as jnp
from jax import lax
from jax.experimental import pallas as pl
from jax.experimental.pallas import tpu as pltpu
from jax.sharding import PartitionSpec as P

F32 = jnp.float32
BF16 = jnp.bfloat16
TAIL = 256
ROOT = math.sqrt(2.0 / math.pi)
CUBE = 0.044715


def dot(a, b, a_dim, b_dim):
    return lax.dot_general(a, b, (((a_dim,), (b_dim,)), ((), ())), preferred_element_type=F32)


def pieces(values):
    high = values.astype(BF16).astype(F32)
    rest = values - high
    middle = rest.astype(BF16).astype(F32)
    return [high, middle, rest - middle]


def stat_block(stats):
    lane = lax.broadcasted_iota(jnp.int32, (stats[0].shape[0], TAIL), 1)
    block = jnp.zeros(lane.shape, F32)
    for i, piece in enumerate([p for s in stats for p in pieces(s)]):
        block = jnp.where(lane == i, piece, block)
    return block


def read_stat(block, i):
    cols = [block[..., k : k + 1].astype(F32) for k in range(3 * i, 3 * i + 3)]
    return cols[0] + cols[1] + cols[2]


def copies_kernel(values, out):
    for i in range(out.shape[0]):
        out[i] = values[...]


def logit_kernel(message, tokens, tokens_other, keys, logits, columns):
    own, width = keys.shape
    keys[...] = message[...].reshape(own, width)
    value = jnp.concatenate(
        [dot(keys[...], tokens[...], 1, 1), dot(keys[...], tokens_other[...], 1, 1)], axis=1
    )
    logits[...] = value
    peak = jnp.max(value, axis=0, keepdims=True)
    columns[0:1, :] = peak
    columns[1:2, :] = jnp.sum(jnp.exp(value - peak), axis=0, keepdims=True)


def dispatch_kernel(logits, tokens, tokens_other, sums, stats):
    count = tokens.shape[0]
    value = logits[...]
    peak = jnp.max(value, axis=1, keepdims=True)
    weights = jnp.exp(value - peak)
    total = jnp.sum(weights, axis=1, keepdims=True)
    weights = weights.astype(BF16)
    part = dot(weights[:, :count], tokens[...], 1, 0)
    part += dot(weights[:, count:], tokens_other[...], 1, 0)
    sums[...] = part.astype(BF16).reshape(sums.shape)
    stats[...] = stat_block([peak, total]).astype(BF16).reshape(stats.shape)


def turn(columns, count):
    return jnp.concatenate([columns[:, count:], columns[:, :count]], axis=1)


def combine_kernel(logits, columns, columns_other, cotangent, cotangent_other, sums, stats, combine, out):
    count, width = cotangent.shape
    other = turn(columns_other[...], count)
    here = columns[...]
    peak = jnp.maximum(here[0:1], other[0:1])
    total = here[1:2] * jnp.exp(here[0:1] - peak) + other[1:2] * jnp.exp(other[0:1] - peak)
    weights = (jnp.exp(logits[...] - peak) / total).astype(BF16)
    combine[...] = weights
    part = dot(weights[:, :count], cotangent[...], 1, 0)
    part += dot(weights[:, count:], cotangent_other[...], 1, 0)
    out[:, :, :width] = sums[...]
    out[:, :, width : 2 * width] = part.astype(BF16).reshape(sums.shape)
    out[:, :, 2 * width :] = stats[...]


def merge(message):
    width = (message.shape[2] - TAIL) // 2
    stats = message[:, :, 2 * width : 2 * width + 128]
    peaks, totals = read_stat(stats, 0), read_stat(stats, 1)
    top = jnp.max(peaks, axis=0, keepdims=True)
    scales = jnp.exp(peaks - top)
    total = jnp.sum(totals * scales, axis=0)
    first = message[0, :, :width].astype(F32) * scales[0]
    for p in range(1, message.shape[0]):
        first += message[p, :, :width].astype(F32) * scales[p]
    second = message[0, :, width : 2 * width].astype(F32)
    for p in range(1, message.shape[0]):
        second += message[p, :, width : 2 * width].astype(F32)
    return first, second, top[0], total


def merge_kernel(message, out):
    width = (message.shape[2] - TAIL) // 2
    first, second, top, total = merge(message)
    first, second = first.astype(BF16), second.astype(BF16)
    block = stat_block([top, total]).astype(BF16)
    for i in range(out.shape[0]):
        out[i, :, :width] = first
        out[i, :, width : 2 * width] = second
        out[i, :, 2 * width :] = block


def expert_kernel(
    message, w_in, w_out, parts, sums, stats, slot_in_out, out_grad_out, hidden_out, pre_grad_out
):
    width = sums.shape[1]
    first, second, top, total = merge(message)
    slot_sum = first / total
    sums[...] = slot_sum
    lane = lax.broadcasted_iota(jnp.int32, stats.shape, 1)
    stats[...] = jnp.where(lane == 0, top, total)
    slot_in = slot_sum.astype(BF16)
    out_grad = second.astype(BF16)
    slot_in_out[...] = slot_in
    out_grad_out[...] = out_grad
    pre_act = dot(slot_in, w_in[...], 1, 0)
    tanh = jnp.tanh(ROOT * (pre_act + CUBE * (pre_act * pre_act * pre_act)))
    hidden = (pre_act * (0.5 * (1.0 + tanh))).astype(BF16)
    hidden_out[...] = hidden
    act_grad = dot(out_grad, w_out[...], 1, 1)
    slope = 0.5 * (1.0 + tanh) + 0.5 * pre_act * (1.0 - tanh * tanh) * (
        ROOT * (1.0 + 3.0 * CUBE * (pre_act * pre_act))
    )
    pre_grad = (act_grad * slope).astype(BF16)
    pre_grad_out[...] = pre_grad
    out_part = dot(hidden, w_out[...], 1, 0).astype(BF16)
    slot_part = dot(pre_grad, w_in[...], 1, 1).astype(BF16)
    for i in range(parts.shape[0]):
        parts[i, :, :width] = out_part
        parts[i, :, width:] = slot_part


def outs_kernel(parts, sums, stats, out):
    width = sums.shape[1]
    total = parts[0].astype(F32)
    for p in range(1, parts.shape[0]):
        total += parts[p].astype(F32)
    values = total.astype(BF16)
    crossing = jnp.sum(values[:, width:].astype(F32) * sums[...], axis=1, keepdims=True)
    block = stat_block([stats[:, 0:1], stats[:, 1:2], crossing]).astype(BF16)
    for i in range(out.shape[0]):
        out[i, :, : 2 * width] = values
        out[i, :, 2 * width :] = block


def combine_dot_kernel(outs, cotangent, cotangent_other, combine, dots, columns):
    width = cotangent.shape[1]
    slot_out = outs[:, :, :width].reshape(combine.shape[0], width)
    value = jnp.concatenate(
        [dot(slot_out, cotangent[...], 1, 1), dot(slot_out, cotangent_other[...], 1, 1)], axis=1
    )
    dots[...] = value
    part = jnp.sum(combine[...].astype(F32) * value, axis=0, keepdims=True)
    columns[...] = jnp.concatenate([part, part], axis=0)


def pick_kernel(outs, tokens, tokens_other, logits, dispatch, term):
    own, width = logits.shape[0], tokens.shape[1]
    block = outs[:, :, 2 * width : 2 * width + 128].reshape(own, 128).astype(F32)
    peak, total, crossing = (read_stat(block, i) for i in range(3))
    weights = (jnp.exp(logits[...] - peak) / total).astype(BF16)
    dispatch[...] = weights
    slot_grad = outs[:, :, width : 2 * width].reshape(own, width)
    value = jnp.concatenate(
        [dot(slot_grad, tokens[...], 1, 1), dot(slot_grad, tokens_other[...], 1, 1)], axis=1
    )
    term[...] = weights.astype(F32) * (value - crossing)


def key_kernel(
    outs, term, dots, combine, columns, columns_other, dispatch, keys, tokens, tokens_other,
    out, pack, weights,
):
    count, width = tokens.shape
    own = keys.shape[0]
    column = columns[0:1, :] + turn(columns_other[...], count)[0:1]
    combine_grad = combine[...].astype(F32) * (dots[...] - column)
    logit_grad = (term[...] + combine_grad).astype(BF16)
    part = dot(logit_grad[:, :count], tokens[...], 1, 0)
    part += dot(logit_grad[:, count:], tokens_other[...], 1, 0)
    out[...] = part.astype(BF16).reshape(out.shape)
    pack[:, :width] = outs[:, :, :width].reshape(own, width)
    pack[:, width : 2 * width] = outs[:, :, width : 2 * width].reshape(own, width)
    pack[:, 2 * width : 3 * width] = keys[...]
    for i, values in enumerate((combine[...], dispatch[...], logit_grad)):
        pack[:, 3 * width + i * count : 3 * width + (i + 1) * count] = values[:, count:]
        weights[:, i * count : (i + 1) * count] = values[:, :count]


def token_kernel(pack, pack_other, weights, slot_out, rest, combine, rest_weights):
    own = pack.shape[0]
    width = slot_out.shape[1]
    count = combine.shape[1]
    other = pack_other[:, 3 * width :]
    slot_out[:own] = pack[:, :width]
    slot_out[own:] = pack_other[:, :width]
    combine[:own] = weights[:, :count]
    combine[own:] = other[:, :count]
    for i in range(2):
        cols = slice((i + 1) * width, (i + 2) * width)
        rest[2 * i * own : (2 * i + 1) * own] = pack[:, cols]
        rest[(2 * i + 1) * own : (2 * i + 2) * own] = pack_other[:, cols]
        cols = slice((i + 1) * count, (i + 2) * count)
        rest_weights[2 * i * own : (2 * i + 1) * own] = weights[:, cols]
        rest_weights[(2 * i + 1) * own : (2 * i + 2) * own] = other[:, cols]


def key_merge_kernel(message, out):
    total = message[0].astype(F32)
    for p in range(1, message.shape[0]):
        total += message[p].astype(F32)
    for i in range(out.shape[0]):
        out[i] = total.astype(out.dtype)


def key_sum_kernel(message, out):
    total = message[0].astype(F32)
    for p in range(1, message.shape[0]):
        total += message[p].astype(F32)
    out[...] = total


def call(kernel, outs, *args, vmem=True):
    whole = pl.BlockSpec(memory_space=pltpu.VMEM)
    make = pltpu.VMEM if vmem else jax.ShapeDtypeStruct
    return pl.pallas_call(
        kernel,
        out_shape=[make(shape, dtype) for shape, dtype in outs],
        in_specs=[whole] * len(args),
        out_specs=[whole] * len(outs),
        compiler_params=pltpu.CompilerParams(vmem_limit_bytes=24 * 1024 * 1024),
    )(*args)


def body(tokens, slot_keys, w_in, w_out, cotangent):
    count, width = tokens.shape
    hidden_units = w_in.shape[2]
    seq = lax.axis_size("seq")
    experts = lax.axis_size("expert")
    rows = slot_keys.shape[0]
    half = experts // 2
    own = half * rows
    both = 2 * count
    long = 2 * width + TAIL
    order = [4 * i + 2 * j for j in range(2) for i in range(half // 2)]
    same_core = [[i + c for i in order] for c in range(2)]
    partner = [(i, i ^ 1) for i in range(experts)]

    def swap(values):
        return lax.ppermute(values, "expert", partner)

    def exchange(values):
        return lax.all_to_all(values, "expert", 0, 0, tiled=True, axis_index_groups=same_core)

    def exchange_seq(values):
        return lax.all_to_all(values, "seq", 0, 0, tiled=True)

    tokens_other, cotangent_other = swap(tokens), swap(cotangent)
    (message,) = call(copies_kernel, [((half, rows, width), BF16)], slot_keys)
    keys, logits, columns = call(
        logit_kernel,
        [((own, width), BF16), ((own, both), F32), ((2, both), F32)],
        exchange(message), tokens, tokens_other,
    )
    columns_other = swap(columns)
    sums, stats = call(
        dispatch_kernel,
        [((half, rows, width), BF16), ((half, rows, TAIL), BF16)],
        logits, tokens, tokens_other,
    )
    combine, message = call(
        combine_kernel,
        [((own, both), BF16), ((half, rows, long), BF16)],
        logits, columns, columns_other, cotangent, cotangent_other, sums, stats,
    )
    (message,) = call(merge_kernel, [((seq, rows, long), BF16)], exchange(message))
    parts, sums, stats, slot_in, out_grad, hidden, pre_grad = call(
        expert_kernel,
        [
            ((seq, rows, 2 * width), BF16),
            ((rows, width), F32),
            ((rows, 128), F32),
            ((rows, width), BF16),
            ((rows, width), BF16),
            ((rows, hidden_units), BF16),
            ((rows, hidden_units), BF16),
        ],
        exchange_seq(message), w_in[0], w_out[0],
    )
    (message,) = call(
        outs_kernel, [((half, rows, long), BF16)], exchange_seq(parts), sums, stats
    )
    outs = exchange(message)
    dots, columns = call(
        combine_dot_kernel,
        [((own, both), F32), ((2, both), F32)],
        outs, cotangent, cotangent_other, combine,
    )
    columns_other = swap(columns)
    dispatch, term = call(
        pick_kernel,
        [((own, both), BF16), ((own, both), F32)],
        outs, tokens, tokens_other, logits,
    )
    message, pack, weights = call(
        key_kernel,
        [
            ((half, rows, width), BF16),
            ((own, 3 * width + 3 * count), BF16),
            ((own, 3 * count), BF16),
        ],
        outs, term, dots, combine, columns, columns_other, dispatch, keys, tokens, tokens_other,
    )
    (message,) = call(key_merge_kernel, [((seq, rows, width), BF16)], exchange(message))
    (key_grad,) = call(key_sum_kernel, [((rows, width), F32)], exchange_seq(message), vmem=False)

    slot_out, rest, combine, rest_weights = call(
        token_kernel,
        [
            ((2 * own, width), BF16),
            ((4 * own, width), BF16),
            ((2 * own, count), BF16),
            ((4 * own, count), BF16),
        ],
        pack, swap(pack), weights,
    )
    w_out_grad = dot(hidden, out_grad, 0, 0).astype(BF16)[None]
    w_in_grad = dot(slot_in, pre_grad, 0, 0).astype(BF16)[None]
    layer_out = dot(combine, slot_out, 0, 0).astype(BF16)
    token_grad = dot(rest_weights, rest, 0, 0).astype(BF16)
    return (layer_out, token_grad, key_grad, w_in_grad, w_out_grad)


def solution(mesh):
    in_specs = (
        P(("seq", "expert"), None),
        P("expert", None),
        P("expert", None, "seq"),
        P("expert", "seq", None),
        P(("seq", "expert"), None),
    )
    out_specs = (
        P(("seq", "expert"), None),
        P(("seq", "expert"), None),
        P("expert", None),
        P("expert", None, "seq"),
        P("expert", "seq", None),
    )
    return jax.shard_map(body, mesh=mesh, in_specs=in_specs, out_specs=out_specs, check_vma=False)
```

time: 137 us -> 131 us (0.956)
  waiting for transfers between devices: 20.3 us -> 14.3 us
  local copies, waits for them, and re-layouts: 3.81 us -> 2.23 us
    ppermute x4 -> x5, waiting for transfers between devices: 6.65 us -> 0.7 us  [swap(): return lax.ppermute(values, 'expert', partner)]
    unnamed x15 -> x12, local copies, waits for them, and re-layouts: 3.81 us -> 2.23 us
    pallas_call x10 -> x13, Pallas kernels: 7.15 us -> 8.52 us  [call(): pl.pallas_call(kernel, out_shape=[make(shape, dtype) for shape, dtype in...]
  transfers between devices with their start and end apart: 6 -> 7, of which waited for: 6 -> 4; matrix products, arithmetic and copies ran while one was open for 5% -> 3% of each run, Pallas kernels for 0% -> 3%
where the time goes in v3:
time: 131 us; the launch traced here: 130 us
  blocking collectives  88.7 us (68%)
  waiting for transfers between devices  14.3 us (11%)
  starting transfers between devices  8.98 us (7%)
  Pallas kernels  8.52 us (7%)
  matrix products  7.02 us (5%)
  local copies, waits for them, and re-layouts  2.23 us (2%)
    all_to_all x3, blocking collectives, exchange(): lax.all_to_all(values, 'expert', 0, 0, tiled=True, axis_index_groups=same...  67.8 us
    all_to_all x2, blocking collectives, exchange_seq(): return lax.all_to_all(values, 'seq', 0, 0, tiled=True)  20.9 us
    all_to_all x1, waiting for transfers between devices, exchange(): lax.all_to_all(values, 'expert', 0, 0, tiled=True, axis_index_groups=same...  10.2 us
    pallas_call x13, Pallas kernels, call(): pl.pallas_call(kernel, out_shape=[make(shape, dtype) for shape, dtype in...  8.52 us
    dot_general x4, matrix products, dot(): lax.dot_general(a, b, (((a_dim,), (b_dim,)), ((), ())), preferred_element...  7.02 us
    all_to_all x1, starting transfers between devices, exchange_seq(): return lax.all_to_all(values, 'seq', 0, 0, tiled=True)  4.5 us
    all_to_all x1, starting transfers between devices, exchange(): lax.all_to_all(values, 'expert', 0, 0, tiled=True, axis_index_groups=same...  3.53 us
    all_to_all x1, waiting for transfers between devices, exchange_seq(): return lax.all_to_all(values, 'seq', 0, 0, tiled=True)  3.38 us
  transfers between devices with their start and end apart: 7, of which 4 were waited for; matrix products, arithmetic and copies ran while one was open for 3% of the time, Pallas kernels for 3%

profile of v3, /device:TPU:2, one launch (start us, length us, event | category | flops | bytes accessed | tf_op | source)
XLA Modules:
  0.0 130.4 jit_solution(15337197860178348755)
XLA Ops:
  0.6 0.1 collective-permute-start
  0.7 0.5 collective-permute-start.2
  1.2 0.0 copy-start.5
  1.2 0.7 copy-done.5
  2.0 22.9 %all_to_all.35.message = bf16[16,2,4096]{2,1,0:T(2,128)(2,1)S(1)} all-to-all(bf16[16,2,4096]{2,1,0:T(2,128)(2,1)S(1)} %shard_map.92), channel_id=1, replica_groups={{0,4,8,12,16,20,24,28,2,6,10,14,18,22,26,30},{1,5,9,13,17,21,25,29,3,7,..., dimensions={0} | all-to-all | bytes 524288 | tf_op jit(solution)/shard_map/all_to_all | solution.py:267
  24.9 0.0 collective-permute-done.tokens_other
  24.9 0.0 copy-start
  24.9 1.2 copy-done
  26.1 0.0 copy-start.1
  26.1 0.0 copy-start.2
  26.1 0.8 shard_map.93
  26.9 0.1 collective-permute-start.1
  27.1 0.3 copy-done.1
  27.3 0.5 shard_map.94
  27.8 0.0 collective-permute-done.2.cotangent_other
  27.8 0.4 collective-permute-done.1.columns_other
  28.2 0.0 copy-done.2
  28.2 0.0 copy-start.3
  28.2 0.0 copy-start.4
  28.2 0.4 shard_map.95
  28.6 24.9 %all_to_all.36.message = bf16[16,2,8448]{2,1,0:T(2,128)(2,1)S(1)} all-to-all(bf16[16,2,8448]{2,1,0:T(2,128)(2,1)S(1)} %get-tuple-element.34), channel_id=1, replica_groups={{0,4,8,12,16,20,24,28,2,6,10,14,18,22,26,30},{1,5,9,13,17,21,25,29,3,7,..., dimensions={0} | all-to-all | bytes 1081344 | tf_op jit(solution)/shard_map/all_to_all | solution.py:267
  53.5 0.3 shard_map.96
  53.8 10.9 %all_to_all.37.message = bf16[8,2,8448]{2,1,0:T(2,128)(2,1)S(1)} all-to-all(bf16[8,2,8448]{2,1,0:T(2,128)(2,1)S(1)} %shard_map.96), channel_id=1, replica_groups=mesh['seq'=8,'expert'=32] {'seq'}, dimensions={0} | all-to-all | bytes 540672 | tf_op jit(solution)/shard_map/all_to_all | solution.py:270
  64.8 0.0 copy-done.3
  64.8 0.0 copy-done.4
  64.8 2.0 %shard_map.97 = (bf16[8,2,8192]{2,1,0:T(2,128)(2,1)S(1)}, f32[2,4096]{1,0:T(2,128)S(1)}, f32[2,128]{1,0:T(2,128)S(1)}, bf16[2,4096]{1,0:T(2,128)(2,1)S(1)}, bf16...) custom-call(bf16[8,2,8448]{2,1,0:T(2,128)(2,1)S(1)} %all_to_all.37.message, ...), custom_call_target="tpu_custom_call" | custom-call | tf_op jit(solution)/shard_map/pallas_call | solution.py:240
  66.8 9.9 %all_to_all.38.parts = bf16[8,2,8192]{2,1,0:T(2,128)(2,1)S(1)} all-to-all(bf16[8,2,8192]{2,1,0:T(2,128)(2,1)S(1)} %get-tuple-element.35), channel_id=1, replica_groups=mesh['seq'=8,'expert'=32] {'seq'}, dimensions={0} | all-to-all | bytes 524288 | tf_op jit(solution)/shard_map/all_to_all | solution.py:270
  76.8 0.2 shard_map.98
  76.9 20.0 %all_to_all.39.outs = bf16[16,2,8448]{2,1,0:T(2,128)(2,1)S(1)} all-to-all(bf16[16,2,8448]{2,1,0:T(2,128)(2,1)S(1)} %shard_map.98), channel_id=1, replica_groups={{0,4,8,12,16,20,24,28,2,6,10,14,18,22,26,30},{1,5,9,13,17,21,25,29,3,7,..., dimensions={0} | all-to-all | bytes 1081344 | tf_op jit(solution)/shard_map/all_to_all | solution.py:267
  96.9 0.8 shard_map.100
  97.7 0.1 collective-permute-start.3
  97.8 0.8 shard_map.99
  98.6 0.3 collective-permute-done.3.columns_other
  98.9 1.2 shard_map.101
  100.1 0.2 collective-permute-start.4
  100.3 3.5 %all-to-all-start.5 = ((bf16[16,2,4096]{2,1,0:T(2,128)(2,1)}), bf16[16,2,4096]{2,1,0:T(2,128)(2,1)S(1)}, u32[]{:S(2)}, u32[]{:S(2)}) async-start(bf16[16,2,4096]{2,1,0:T(2,128)(2,1)} %get-tuple-element.50), calls=%async_computation.5 | async-start | bytes 524288 | tf_op jit(solution)/shard_map/all_to_all | solution.py:267
  103.8 2.1 %fusion = bf16[1,4096,256]{2,1,0:T(8,128)(2,1)} fusion(bf16[2,4096]{1,0:T(2,128)(2,1)S(1)} %get-tuple-element.51, bf16[2,256]{1,0:T(2,128)(2,1)S(1)} %get-tuple-element.52), kind=kOutput, calls=%fused_computation.2 | convolution fusion | flops 5242880 | bytes 2114560 | tf_op jit(solution)/shard_map/dot_general | solution.py:18
  105.9 10.2 %all-to-all-done.5.message = bf16[16,2,4096]{2,1,0:T(2,128)(2,1)S(1)} async-done(((bf16[16,2,4096]{2,1,0:T(2,128)(2,1)}), bf16[16,2,4096]{2,1,0:T(2,128)(2,1)S(1)}, u32[]{:S(2)}, u32[]{:S(2)}) %all-to-all-start.5) | async-done | bytes 262176 | tf_op jit(solution)/shard_map/all_to_all | solution.py:267
  116.1 0.7 shard_map.103
  116.8 4.5 %all-to-all-start.6 = ((bf16[8,2,4096]{2,1,0:T(2,128)(2,1)}), bf16[8,2,4096]{2,1,0:T(2,128)(2,1)S(1)}, u32[]{:S(2)}, u32[]{:S(2)}) async-start(bf16[8,2,4096]{2,1,0:T(2,128)(2,1)} %shard_map.103), calls=%async_computation.6 | async-start | bytes 262144 | tf_op jit(solution)/shard_map/all_to_all | solution.py:270
  121.3 2.1 %fusion.1 = bf16[1,256,4096]{2,1,0:T(8,128)(2,1)} fusion(bf16[2,256]{1,0:T(2,128)(2,1)S(1)} %get-tuple-element.53, bf16[2,4096]{1,0:T(2,128)(2,1)S(1)} %get-tuple-element.54), kind=kOutput, calls=%fused_computation.3 | convolution fusion | flops 5242880 | bytes 2114560 | tf_op jit(solution)/shard_map/dot_general | solution.py:18
  123.4 3.4 %all-to-all-done.6.message = bf16[8,2,4096]{2,1,0:T(2,128)(2,1)S(1)} async-done(((bf16[8,2,4096]{2,1,0:T(2,128)(2,1)}), bf16[8,2,4096]{2,1,0:T(2,128)(2,1)S(1)}, u32[]{:S(2)}, u32[]{:S(2)}) %all-to-all-start.6) | async-done | bytes 131104 | tf_op jit(solution)/shard_map/all_to_all | solution.py:270
  126.8 0.6 shard_map.104
  127.4 0.0 collective-permute-done.4.pack_other
  127.4 0.1 shard_map.102
  127.5 1.4 %convolution_convert_fusion.3 = bf16[128,4096]{1,0:T(8,128)(2,1)} fusion(bf16[64,128]{1,0:T(8,128)(2,1)S(1)} %get-tuple-element.46, bf16[64,4096]{1,0:T(8,128)(2,1)S(1)} %get-tuple-element.47), kind=kOutput, calls=%fused_computation.5 | convolution fusion | flops 67633152 | bytes 1589248 | tf_op jit(solution)/shard_map/dot_general | solution.py:18
  128.9 1.4 %convolution_convert_fusion.2 = bf16[128,4096]{1,0:T(8,128)(2,1)} fusion(bf16[128,128]{1,0:T(8,128)(2,1)S(1)} %get-tuple-element.48, bf16[128,4096]{1,0:T(8,128)(2,1)S(1)} %get-tuple-element.49), kind=kOutput, calls=%fused_computation.4 | convolution fusion | flops 134742016 | bytes 2129920 | tf_op jit(solution)/shard_map/dot_general | solution.py:18
  (1 shorter events, 0.0 us)
Async XLA Ops:
  0.6 24.2 %collective-permute-start = (bf16[128,4096]{1,0:T(8,128)(2,1)}, bf16[128,4096]{1,0:T(8,128)(2,1)S(1)}, u32[]{:S(2)}, u32[]{:S(2)}) collective-permute-start(bf16[128,4096]{1,0:T(8,128)(2,1)} %tokens.7), channel_id=1, source_target_pairs={{0,1},{1,0},{2,3},{3,2},{4,5},{5,4},{6,7},{7,6},{8,9},{9,8},{10,11... | collective-permute-start | bytes 3145736 | tf_op jit(solution)/shard_map/ppermute | solution.py:264
  0.7 27.1 %collective-permute-start.2 = (bf16[128,4096]{1,0:T(8,128)(2,1)}, bf16[128,4096]{1,0:T(8,128)(2,1)S(1)}, u32[]{:S(2)}, u32[]{:S(2)}) collective-permute-start(bf16[128,4096]{1,0:T(8,128)(2,1)} %cotangent.3), channel_id=1, source_target_pairs={{0,1},{1,0},{2,3},{3,2},{4,5},{5,4},{6,7},{7,6},{8,9},{9,8},{10,11... | collective-permute-start | bytes 3145736 | tf_op jit(solution)/shard_map/ppermute | solution.py:264
  1.2 0.7 copy-start.5
  24.9 1.2 copy-start
  26.1 1.2 copy-start.1
  26.1 2.1 %copy-start.2 = (bf16[128,4096]{1,0:T(8,128)(2,1)S(1)}, bf16[128,4096]{1,0:T(8,128)(2,1)}, u32[]{:S(2)}) copy-start(bf16[128,4096]{1,0:T(8,128)(2,1)} %cotangent.3) | copy-start | bytes 3145732
  26.9 1.2 collective-permute-start.1
  28.2 36.6 %copy-start.3 = (bf16[1,4096,256]{2,1,0:T(8,128)(2,1)S(1)}, bf16[1,4096,256]{2,1,0:T(8,128)(2,1)}, u32[]{:S(2)}) copy-start(bf16[1,4096,256]{2,1,0:T(8,128)(2,1)} %param.7) | copy-start | bytes 6291460
  28.2 36.6 %copy-start.4 = (bf16[1,256,4096]{2,1,0:T(8,128)(2,1)S(1)}, bf16[1,256,4096]{2,1,0:T(8,128)(2,1)}, u32[]{:S(2)}) copy-start(bf16[1,256,4096]{2,1,0:T(8,128)(2,1)} %param.8) | copy-start | bytes 6291460
  97.7 1.2 collective-permute-start.3
  100.1 27.3 %collective-permute-start.4 = (bf16[32,12672]{1,0:T(8,128)(2,1)S(1)}, bf16[32,12672]{1,0:T(8,128)(2,1)S(1)}, u32[]{:S(2)}, u32[]{:S(2)}) collective-permute-start(bf16[32,12672]{1,0:T(8,128)(2,1)S(1)} %get-tuple-element.44.pack), channel_id=1, source_target_pairs={{0,1},{1,0},{2,3},{3,2},{4,5},{5,4},{6,7},{7,6},{8,9},{9,8},{10,11... | collective-permute-start | bytes 2433032 | tf_op jit(solution)/shard_map/ppermute | solution.py:264
  100.3 15.8 %all-to-all-start.5 = ((bf16[16,2,4096]{2,1,0:T(2,128)(2,1)}), bf16[16,2,4096]{2,1,0:T(2,128)(2,1)S(1)}, u32[]{:S(2)}, u32[]{:S(2)}) async-start(bf16[16,2,4096]{2,1,0:T(2,128)(2,1)} %get-tuple-element.50), calls=%async_computation.5 | async-start | bytes 524288 | tf_op jit(solution)/shard_map/all_to_all | solution.py:267
  116.8 10.0 %all-to-all-start.6 = ((bf16[8,2,4096]{2,1,0:T(2,128)(2,1)}), bf16[8,2,4096]{2,1,0:T(2,128)(2,1)S(1)}, u32[]{:S(2)}, u32[]{:S(2)}) async-start(bf16[8,2,4096]{2,1,0:T(2,128)(2,1)} %shard_map.103), calls=%async_computation.6 | async-start | bytes 262144 | tf_op jit(solution)/shard_map/all_to_all | solution.py:270

commit v4 on v3

--- a/solution.py
+++ b/solution.py
@@ -36,6 +36,11 @@
 def read_stat(block, i):
     cols = [block[..., k : k + 1].astype(F32) for k in range(3 * i, 3 * i + 3)]
     return cols[0] + cols[1] + cols[2]
+
+
+def bit_reversed(size):
+    bits = size.bit_length() - 1
+    return sorted(range(size), key=lambda i: [i >> k & 1 for k in range(bits)])
 
 
 def copies_kernel(values, out):
@@ -182,26 +187,33 @@
 
 
 def key_kernel(
-    outs, term, dots, combine, columns, columns_other, dispatch, keys, tokens, tokens_other,
-    out, pack, weights,
+    term, dots, combine, columns, columns_other, tokens, tokens_other, out, logit_grad_out
 ):
-    count, width = tokens.shape
-    own = keys.shape[0]
+    count = tokens.shape[0]
     column = columns[0:1, :] + turn(columns_other[...], count)[0:1]
     combine_grad = combine[...].astype(F32) * (dots[...] - column)
     logit_grad = (term[...] + combine_grad).astype(BF16)
     part = dot(logit_grad[:, :count], tokens[...], 1, 0)
     part += dot(logit_grad[:, count:], tokens_other[...], 1, 0)
     out[...] = part.astype(BF16).reshape(out.shape)
+    logit_grad_out[...] = logit_grad
+
+
+def pack_kernel(outs, keys, combine, dispatch, logit_grad, pack, weights):
+    own, width = keys.shape
+    count = weights.shape[1] // 3
     pack[:, :width] = outs[:, :, :width].reshape(own, width)
     pack[:, width : 2 * width] = outs[:, :, width : 2 * width].reshape(own, width)
     pack[:, 2 * width : 3 * width] = keys[...]
-    for i, values in enumerate((combine[...], dispatch[...], logit_grad)):
+    for i, values in enumerate((combine[...], dispatch[...], logit_grad[...])):
         pack[:, 3 * width + i * count : 3 * width + (i + 1) * count] = values[:, count:]
         weights[:, i * count : (i + 1) * count] = values[:, :count]
 
 
-def token_kernel(pack, pack_other, weights, slot_out, rest, combine, rest_weights):
+def token_kernel(pack, pack_other, weights, *refs):
+    slot_out, rest, combine, rest_weights = refs[4:8]
+    for here, there in zip(refs[:4], refs[8:]):
+        there[...] = here[...]
     own = pack.shape[0]
     width = slot_out.shape[1]
     count = combine.shape[1]
@@ -219,7 +231,8 @@
         rest_weights[(2 * i + 1) * own : (2 * i + 2) * own] = other[:, cols]
 
 
-def key_merge_kernel(message, out):
+def key_merge_kernel(message, *refs):
+    out = refs[-1]
     total = message[0].astype(F32)
     for p in range(1, message.shape[0]):
         total += message[p].astype(F32)
@@ -234,13 +247,18 @@
     out[...] = total
 
 
-def call(kernel, outs, *args, vmem=True):
+def call(kernel, outs, *args, vmem=True, far=()):
     whole = pl.BlockSpec(memory_space=pltpu.VMEM)
+    there = pl.BlockSpec(memory_space=pltpu.HBM)
     make = pltpu.VMEM if vmem else jax.ShapeDtypeStruct
+    args = [
+        pltpu.with_memory_space_constraint(a, pltpu.HBM) if i in far else a
+        for i, a in enumerate(args)
+    ]
     return pl.pallas_call(
         kernel,
         out_shape=[make(shape, dtype) for shape, dtype in outs],
-        in_specs=[whole] * len(args),
+        in_specs=[there if i in far else whole for i in range(len(args))],
         out_specs=[whole] * len(outs),
         compiler_params=pltpu.CompilerParams(vmem_limit_bytes=24 * 1024 * 1024),
     )(*args)
@@ -256,7 +274,7 @@
     own = half * rows
     both = 2 * count
     long = 2 * width + TAIL
-    order = [4 * i + 2 * j for j in range(2) for i in range(half // 2)]
+    order = [4 * i + 2 * j for j in range(2) for i in bit_reversed(half // 2)]
     same_core = [[i + c for i in order] for c in range(2)]
     partner = [(i, i ^ 1) for i in range(experts)]
 
@@ -316,32 +334,39 @@
         [((own, both), BF16), ((own, both), F32)],
         outs, tokens, tokens_other, logits,
     )
-    message, pack, weights = call(
+    message, logit_grad = call(
         key_kernel,
-        [
-            ((half, rows, width), BF16),
-            ((own, 3 * width + 3 * count), BF16),
-            ((own, 3 * count), BF16),
-        ],
-        outs, term, dots, combine, columns, columns_other, dispatch, keys, tokens, tokens_other,
-    )
-    (message,) = call(key_merge_kernel, [((seq, rows, width), BF16)], exchange(message))
-    (key_grad,) = call(key_sum_kernel, [((rows, width), F32)], exchange_seq(message), vmem=False)
-
-    slot_out, rest, combine, rest_weights = call(
+        [((half, rows, width), BF16), ((own, both), BF16)],
+        term, dots, combine, columns, columns_other, tokens, tokens_other,
+    )
+    message = exchange(message)
+    pack, weights = call(
+        pack_kernel,
+        [((own, 3 * width + 3 * count), BF16), ((own, 3 * count), BF16)],
+        outs, keys, combine, dispatch, logit_grad,
+    )
+    factors = (slot_in, out_grad, hidden, pre_grad)
+    slot_out, rest, combine, rest_weights, slot_in, out_grad, hidden, pre_grad = call(
         token_kernel,
         [
             ((2 * own, width), BF16),
             ((4 * own, width), BF16),
             ((2 * own, count), BF16),
             ((4 * own, count), BF16),
-        ],
-        pack, swap(pack), weights,
-    )
+        ]
+        + [(v.shape, v.dtype) for v in factors],
+        pack, swap(pack), weights, *factors,
+    )
+    layer_out = dot(combine, slot_out, 0, 0).astype(BF16)
+    token_grad = dot(rest_weights, rest, 0, 0).astype(BF16)
     w_out_grad = dot(hidden, out_grad, 0, 0).astype(BF16)[None]
     w_in_grad = dot(slot_in, pre_grad, 0, 0).astype(BF16)[None]
-    layer_out = dot(combine, slot_out, 0, 0).astype(BF16)
-    token_grad = dot(rest_weights, rest, 0, 0).astype(BF16)
+    results = (layer_out, token_grad, w_in_grad, w_out_grad)
+    (message,) = call(
+        key_merge_kernel, [((seq, rows, width), BF16)], message, *results, far=(1, 2, 3, 4)
+    )
+    (key_grad,) = call(key_sum_kernel, [((rows, width), F32)], exchange_seq(message), vmem=False)
+
     return (layer_out, token_grad, key_grad, w_in_grad, w_out_grad)
 
 

time: 131 us -> 128 us (0.977)
  blocking collectives: 88.7 us -> 98 us
  waiting for transfers between devices: 14.3 us -> 7.51 us
  starting transfers between devices: 8.98 us -> 4.57 us
    all_to_all x2 -> x3, blocking collectives: 20.9 us -> 29.9 us  [exchange_seq(): return lax.all_to_all(values, 'seq', 0, 0, tiled=True)]
    all_to_all x1 -> x0, starting transfers between devices: 4.5 us -> none  [exchange_seq(): return lax.all_to_all(values, 'seq', 0, 0, tiled=True)]
    all_to_all x1 -> x0, waiting for transfers between devices: 3.38 us -> none  [exchange_seq(): return lax.all_to_all(values, 'seq', 0, 0, tiled=True)]
    all_to_all x1, waiting for transfers between devices: 10.2 us -> 6.81 us  [exchange(): lax.all_to_all(values, 'expert', 0, 0, tiled=True, axis_index_groups=same...]
    pallas_call x13 -> x14, Pallas kernels: 8.52 us -> 7.9 us  [call(): pl.pallas_call(kernel, out_shape=[make(shape, dtype) for shape, dtype in...]
  transfers between devices with their start and end apart: 7 -> 6, of which waited for: 4 -> 3; matrix products, arithmetic and copies ran while one was open for 3% -> 5% of each run, Pallas kernels for 3% -> 2%
where the time goes in v4:
time: 128 us
  blocking collectives  98 us (77%)
  Pallas kernels  7.9 us (6%)
  waiting for transfers between devices  7.51 us (6%)
  matrix products  7.02 us (5%)
  starting transfers between devices  4.57 us (4%)
  local copies, waits for them, and re-layouts  2.23 us (2%)
    all_to_all x3, blocking collectives, exchange(): lax.all_to_all(values, 'expert', 0, 0, tiled=True, axis_index_groups=same...  68.1 us
    all_to_all x3, blocking collectives, exchange_seq(): return lax.all_to_all(values, 'seq', 0, 0, tiled=True)  29.9 us
    pallas_call x14, Pallas kernels, call(): pl.pallas_call(kernel, out_shape=[make(shape, dtype) for shape, dtype in...  7.9 us
    dot_general x4, matrix products, dot(): lax.dot_general(a, b, (((a_dim,), (b_dim,)), ((), ())), preferred_element...  7.02 us
    all_to_all x1, waiting for transfers between devices, exchange(): lax.all_to_all(values, 'expert', 0, 0, tiled=True, axis_index_groups=same...  6.81 us
    all_to_all x1, starting transfers between devices, exchange(): lax.all_to_all(values, 'expert', 0, 0, tiled=True, axis_index_groups=same...  3.53 us
  transfers between devices with their start and end apart: 6, of which 3 were waited for; matrix products, arithmetic and copies ran while one was open for 5% of the time, Pallas kernels for 2%

profile of v4, /device:TPU:2, one launch (start us, length us, event | category | flops | bytes accessed | tf_op | source)
XLA Modules:
  0.0 127.9 jit_solution(15937364754339480878)
XLA Ops:
  0.6 0.1 collective-permute-start
  0.7 0.5 collective-permute-start.2
  1.2 0.0 copy-start.5
  1.2 0.7 copy-done.5
  2.0 24.7 %all_to_all.35.message = bf16[16,2,4096]{2,1,0:T(2,128)(2,1)S(1)} all-to-all(bf16[16,2,4096]{2,1,0:T(2,128)(2,1)S(1)} %shard_map.92), channel_id=1, replica_groups={{0,16,8,24,4,20,12,28,2,18,10,26,6,22,14,30},{1,17,9,25,5,21,13,29,3,19..., dimensions={0} | all-to-all | bytes 524288 | tf_op jit(solution)/shard_map/all_to_all | solution.py:285
  26.6 0.0 collective-permute-done.tokens_other
  26.6 0.0 copy-start
  26.6 1.2 copy-done
  27.8 0.0 copy-start.1
  27.9 0.0 copy-start.2
  27.9 0.8 shard_map.93
  28.7 0.1 collective-permute-start.1
  28.8 0.3 copy-done.1
  29.1 0.5 shard_map.94
  29.6 0.0 collective-permute-done.2.cotangent_other
  29.6 0.4 collective-permute-done.1.columns_other
  29.9 0.0 copy-done.2
  29.9 0.0 copy-start.3
  29.9 0.0 copy-start.4
  29.9 0.4 shard_map.95
  30.4 23.5 %all_to_all.36.message = bf16[16,2,8448]{2,1,0:T(2,128)(2,1)S(1)} all-to-all(bf16[16,2,8448]{2,1,0:T(2,128)(2,1)S(1)} %get-tuple-element.39), channel_id=1, replica_groups={{0,16,8,24,4,20,12,28,2,18,10,26,6,22,14,30},{1,17,9,25,5,21,13,29,3,19..., dimensions={0} | all-to-all | bytes 1081344 | tf_op jit(solution)/shard_map/all_to_all | solution.py:285
  53.9 0.3 shard_map.96
  54.2 10.9 %all_to_all.37.message = bf16[8,2,8448]{2,1,0:T(2,128)(2,1)S(1)} all-to-all(bf16[8,2,8448]{2,1,0:T(2,128)(2,1)S(1)} %shard_map.96), channel_id=1, replica_groups=mesh['seq'=8,'expert'=32] {'seq'}, dimensions={0} | all-to-all | bytes 540672 | tf_op jit(solution)/shard_map/all_to_all | solution.py:288
  65.1 0.0 copy-done.3
  65.1 0.0 copy-done.4
  65.1 2.0 %shard_map.97 = (bf16[8,2,8192]{2,1,0:T(2,128)(2,1)S(1)}, f32[2,4096]{1,0:T(2,128)S(1)}, f32[2,128]{1,0:T(2,128)S(1)}, bf16[2,4096]{1,0:T(2,128)(2,1)S(1)}, bf16...) custom-call(bf16[8,2,8448]{2,1,0:T(2,128)(2,1)S(1)} %all_to_all.37.message, ...), custom_call_target="tpu_custom_call" | custom-call | tf_op jit(solution)/shard_map/pallas_call | solution.py:258
  67.2 9.9 %all_to_all.38.parts = bf16[8,2,8192]{2,1,0:T(2,128)(2,1)S(1)} all-to-all(bf16[8,2,8192]{2,1,0:T(2,128)(2,1)S(1)} %get-tuple-element.40), channel_id=1, replica_groups=mesh['seq'=8,'expert'=32] {'seq'}, dimensions={0} | all-to-all | bytes 524288 | tf_op jit(solution)/shard_map/all_to_all | solution.py:288
  77.1 0.2 shard_map.98
  77.3 19.9 %all_to_all.39.outs = bf16[16,2,8448]{2,1,0:T(2,128)(2,1)S(1)} all-to-all(bf16[16,2,8448]{2,1,0:T(2,128)(2,1)S(1)} %shard_map.98), channel_id=1, replica_groups={{0,16,8,24,4,20,12,28,2,18,10,26,6,22,14,30},{1,17,9,25,5,21,13,29,3,19..., dimensions={0} | all-to-all | bytes 1081344 | tf_op jit(solution)/shard_map/all_to_all | solution.py:285
  97.2 0.8 shard_map.100
  98.0 0.1 collective-permute-start.3
  98.1 0.8 shard_map.99
  98.9 0.3 collective-permute-done.3.columns_other
  99.2 1.1 shard_map.101
  100.3 0.1 shard_map.102
  100.4 0.3 collective-permute-start.4
  100.7 3.5 %all-to-all-start.5 = ((bf16[16,2,4096]{2,1,0:T(2,128)(2,1)}), bf16[16,2,4096]{2,1,0:T(2,128)(2,1)S(1)}, u32[]{:S(2)}, u32[]{:S(2)}) async-start(bf16[16,2,4096]{2,1,0:T(2,128)(2,1)} %get-tuple-element.60), calls=%async_computation.5 | async-start | bytes 524288 | tf_op jit(solution)/shard_map/all_to_all | solution.py:285
  104.2 0.0 collective-permute-done.4.pack_other
  104.2 0.1 shard_map.103
  104.4 2.1 %fusion.refs_2_ = bf16[1,4096,256]{2,1,0:T(8,128)(2,1)} fusion(bf16[2,4096]{1,0:T(2,128)(2,1)S(1)} %get-tuple-element.61, bf16[2,256]{1,0:T(2,128)(2,1)S(1)} %get-tuple-element.62), kind=kOutput, calls=%fused_computation.2 | convolution fusion | flops 5242880 | bytes 2114560 | tf_op jit(solution)/shard_map/dot_general | solution.py:18
  106.4 2.1 %fusion.1.refs_3_ = bf16[1,256,4096]{2,1,0:T(8,128)(2,1)} fusion(bf16[2,256]{1,0:T(2,128)(2,1)S(1)} %get-tuple-element.63, bf16[2,4096]{1,0:T(2,128)(2,1)S(1)} %get-tuple-element.64), kind=kOutput, calls=%fused_computation.3 | convolution fusion | flops 5242880 | bytes 2114560 | tf_op jit(solution)/shard_map/dot_general | solution.py:18
  108.5 1.4 %convolution_convert_fusion.3.refs_0_ = bf16[128,4096]{1,0:T(8,128)(2,1)} fusion(bf16[64,128]{1,0:T(8,128)(2,1)S(1)} %get-tuple-element.56, bf16[64,4096]{1,0:T(8,128)(2,1)S(1)} %get-tuple-element.57), kind=kOutput, calls=%fused_computation.5 | convolution fusion | flops 67633152 | bytes 1589248 | tf_op jit(solution)/shard_map/dot_general | solution.py:18
  109.9 1.4 %convolution_convert_fusion.2.refs_1_ = bf16[128,4096]{1,0:T(8,128)(2,1)} fusion(bf16[128,128]{1,0:T(8,128)(2,1)S(1)} %get-tuple-element.58, bf16[128,4096]{1,0:T(8,128)(2,1)S(1)} %get-tuple-element.59), kind=kOutput, calls=%fused_computation.4 | convolution fusion | flops 134742016 | bytes 2129920 | tf_op jit(solution)/shard_map/dot_general | solution.py:18
  111.4 6.8 %all-to-all-done.5.message = bf16[16,2,4096]{2,1,0:T(2,128)(2,1)S(1)} async-done(((bf16[16,2,4096]{2,1,0:T(2,128)(2,1)}), bf16[16,2,4096]{2,1,0:T(2,128)(2,1)S(1)}, u32[]{:S(2)}, u32[]{:S(2)}) %all-to-all-start.5) | async-done | bytes 262176 | tf_op jit(solution)/shard_map/all_to_all | solution.py:285
  118.2 0.1 shard_map.104
  118.3 9.1 %all_to_all.40.message = bf16[8,2,4096]{2,1,0:T(2,128)(2,1)S(1)} all-to-all(bf16[8,2,4096]{2,1,0:T(2,128)(2,1)S(1)} %shard_map.104), channel_id=1, replica_groups=mesh['seq'=8,'expert'=32] {'seq'}, dimensions={0} | all-to-all | bytes 262144 | tf_op jit(solution)/shard_map/all_to_all | solution.py:288
  127.3 0.6 shard_map.105
  (1 shorter events, 0.0 us)
Async XLA Ops:
  0.6 26.0 %collective-permute-start = (bf16[128,4096]{1,0:T(8,128)(2,1)}, bf16[128,4096]{1,0:T(8,128)(2,1)S(1)}, u32[]{:S(2)}, u32[]{:S(2)}) collective-permute-start(bf16[128,4096]{1,0:T(8,128)(2,1)} %tokens.7), channel_id=1, source_target_pairs={{0,1},{1,0},{2,3},{3,2},{4,5},{5,4},{6,7},{7,6},{8,9},{9,8},{10,11... | collective-permute-start | bytes 3145736 | tf_op jit(solution)/shard_map/ppermute | solution.py:282
  0.7 28.8 %collective-permute-start.2 = (bf16[128,4096]{1,0:T(8,128)(2,1)}, bf16[128,4096]{1,0:T(8,128)(2,1)S(1)}, u32[]{:S(2)}, u32[]{:S(2)}) collective-permute-start(bf16[128,4096]{1,0:T(8,128)(2,1)} %cotangent.3), channel_id=1, source_target_pairs={{0,1},{1,0},{2,3},{3,2},{4,5},{5,4},{6,7},{7,6},{8,9},{9,8},{10,11... | collective-permute-start | bytes 3145736 | tf_op jit(solution)/shard_map/ppermute | solution.py:282
  1.2 0.7 copy-start.5
  26.6 1.2 copy-start
  27.8 1.2 copy-start.1
  27.9 2.1 %copy-start.2 = (bf16[128,4096]{1,0:T(8,128)(2,1)S(1)}, bf16[128,4096]{1,0:T(8,128)(2,1)}, u32[]{:S(2)}) copy-start(bf16[128,4096]{1,0:T(8,128)(2,1)} %cotangent.3) | copy-start | bytes 3145732
  28.7 1.2 collective-permute-start.1
  29.9 35.2 %copy-start.3 = (bf16[1,4096,256]{2,1,0:T(8,128)(2,1)S(1)}, bf16[1,4096,256]{2,1,0:T(8,128)(2,1)}, u32[]{:S(2)}) copy-start(bf16[1,4096,256]{2,1,0:T(8,128)(2,1)} %param.7) | copy-start | bytes 6291460
  29.9 35.2 %copy-start.4 = (bf16[1,256,4096]{2,1,0:T(8,128)(2,1)S(1)}, bf16[1,256,4096]{2,1,0:T(8,128)(2,1)}, u32[]{:S(2)}) copy-start(bf16[1,256,4096]{2,1,0:T(8,128)(2,1)} %param.8) | copy-start | bytes 6291460
  98.0 1.2 collective-permute-start.3
  100.4 3.8 %collective-permute-start.4 = (bf16[32,12672]{1,0:T(8,128)(2,1)S(1)}, bf16[32,12672]{1,0:T(8,128)(2,1)S(1)}, u32[]{:S(2)}, u32[]{:S(2)}) collective-permute-start(bf16[32,12672]{1,0:T(8,128)(2,1)S(1)} %get-tuple-element.50.pack), channel_id=1, source_target_pairs={{0,1},{1,0},{2,3},{3,2},{4,5},{5,4},{6,7},{7,6},{8,9},{9,8},{10,11... | collective-permute-start | bytes 2433032 | tf_op jit(solution)/shard_map/ppermute | solution.py:282
  100.7 17.5 %all-to-all-start.5 = ((bf16[16,2,4096]{2,1,0:T(2,128)(2,1)}), bf16[16,2,4096]{2,1,0:T(2,128)(2,1)S(1)}, u32[]{:S(2)}, u32[]{:S(2)}) async-start(bf16[16,2,4096]{2,1,0:T(2,128)(2,1)} %get-tuple-element.60), calls=%async_computation.5 | async-start | bytes 524288 | tf_op jit(solution)/shard_map/all_to_all | solution.py:285

commit v5 on v4

--- a/solution.py
+++ b/solution.py
@@ -38,37 +38,33 @@
     return cols[0] + cols[1] + cols[2]
 
 
-def bit_reversed(size):
-    bits = size.bit_length() - 1
-    return sorted(range(size), key=lambda i: [i >> k & 1 for k in range(bits)])
-
-
 def copies_kernel(values, out):
     for i in range(out.shape[0]):
         out[i] = values[...]
 
 
-def logit_kernel(message, tokens, tokens_other, keys, logits, columns):
+def logit_kernel(message, tokens, tokens_other, keys, logits, columns, tokens_both):
     own, width = keys.shape
+    count = tokens.shape[0]
     keys[...] = message[...].reshape(own, width)
-    value = jnp.concatenate(
-        [dot(keys[...], tokens[...], 1, 1), dot(keys[...], tokens_other[...], 1, 1)], axis=1
-    )
+    tokens_both[:count] = tokens[...]
+    tokens_both[count:] = tokens_other[...]
+    value = dot(keys[...], tokens_both[...], 1, 1)
     logits[...] = value
     peak = jnp.max(value, axis=0, keepdims=True)
     columns[0:1, :] = peak
     columns[1:2, :] = jnp.sum(jnp.exp(value - peak), axis=0, keepdims=True)
 
 
-def dispatch_kernel(logits, tokens, tokens_other, sums, stats):
-    count = tokens.shape[0]
+def dispatch_kernel(logits, tokens_both, cotangent, cotangent_other, sums, stats, cotangent_both):
+    count = cotangent.shape[0]
+    cotangent_both[:count] = cotangent[...]
+    cotangent_both[count:] = cotangent_other[...]
     value = logits[...]
     peak = jnp.max(value, axis=1, keepdims=True)
     weights = jnp.exp(value - peak)
     total = jnp.sum(weights, axis=1, keepdims=True)
-    weights = weights.astype(BF16)
-    part = dot(weights[:, :count], tokens[...], 1, 0)
-    part += dot(weights[:, count:], tokens_other[...], 1, 0)
+    part = dot(weights.astype(BF16), tokens_both[...], 1, 0)
     sums[...] = part.astype(BF16).reshape(sums.shape)
     stats[...] = stat_block([peak, total]).astype(BF16).reshape(stats.shape)
 
@@ -77,16 +73,15 @@
     return jnp.concatenate([columns[:, count:], columns[:, :count]], axis=1)
 
 
-def combine_kernel(logits, columns, columns_other, cotangent, cotangent_other, sums, stats, combine, out):
-    count, width = cotangent.shape
+def combine_kernel(logits, columns, columns_other, cotangent_both, sums, stats, combine, out):
+    count, width = cotangent_both.shape[0] // 2, cotangent_both.shape[1]
     other = turn(columns_other[...], count)
     here = columns[...]
     peak = jnp.maximum(here[0:1], other[0:1])
     total = here[1:2] * jnp.exp(here[0:1] - peak) + other[1:2] * jnp.exp(other[0:1] - peak)
     weights = (jnp.exp(logits[...] - peak) / total).astype(BF16)
     combine[...] = weights
-    part = dot(weights[:, :count], cotangent[...], 1, 0)
-    part += dot(weights[:, count:], cotangent_other[...], 1, 0)
+    part = dot(weights, cotangent_both[...], 1, 0)
     out[:, :, :width] = sums[...]
     out[:, :, width : 2 * width] = part.astype(BF16).reshape(sums.shape)
     out[:, :, 2 * width :] = stats[...]
@@ -162,39 +157,34 @@
         out[i, :, 2 * width :] = block
 
 
-def combine_dot_kernel(outs, cotangent, cotangent_other, combine, dots, columns):
-    width = cotangent.shape[1]
+def combine_dot_kernel(outs, cotangent_both, combine, dots, columns):
+    width = cotangent_both.shape[1]
     slot_out = outs[:, :, :width].reshape(combine.shape[0], width)
-    value = jnp.concatenate(
-        [dot(slot_out, cotangent[...], 1, 1), dot(slot_out, cotangent_other[...], 1, 1)], axis=1
-    )
+    value = dot(slot_out, cotangent_both[...], 1, 1)
     dots[...] = value
     part = jnp.sum(combine[...].astype(F32) * value, axis=0, keepdims=True)
     columns[...] = jnp.concatenate([part, part], axis=0)
 
 
-def pick_kernel(outs, tokens, tokens_other, logits, dispatch, term):
-    own, width = logits.shape[0], tokens.shape[1]
+def pick_kernel(outs, tokens_both, logits, dispatch, term):
+    own, width = logits.shape[0], tokens_both.shape[1]
     block = outs[:, :, 2 * width : 2 * width + 128].reshape(own, 128).astype(F32)
     peak, total, crossing = (read_stat(block, i) for i in range(3))
     weights = (jnp.exp(logits[...] - peak) / total).astype(BF16)
     dispatch[...] = weights
     slot_grad = outs[:, :, width : 2 * width].reshape(own, width)
-    value = jnp.concatenate(
-        [dot(slot_grad, tokens[...], 1, 1), dot(slot_grad, tokens_other[...], 1, 1)], axis=1
-    )
+    value = dot(slot_grad, tokens_both[...], 1, 1)
     term[...] = weights.astype(F32) * (value - crossing)
 
 
 def key_kernel(
-    term, dots, combine, columns, columns_other, tokens, tokens_other, out, logit_grad_out
+    term, dots, combine, columns, columns_other, tokens_both, out, logit_grad_out
 ):
-    count = tokens.shape[0]
+    count = tokens_both.shape[0] // 2
     column = columns[0:1, :] + turn(columns_other[...], count)[0:1]
     combine_grad = combine[...].astype(F32) * (dots[...] - column)
     logit_grad = (term[...] + combine_grad).astype(BF16)
-    part = dot(logit_grad[:, :count], tokens[...], 1, 0)
-    part += dot(logit_grad[:, count:], tokens_other[...], 1, 0)
+    part = dot(logit_grad, tokens_both[...], 1, 0)
     out[...] = part.astype(BF16).reshape(out.shape)
     logit_grad_out[...] = logit_grad
 
@@ -274,7 +264,8 @@
     own = half * rows
     both = 2 * count
     long = 2 * width + TAIL
-    order = [4 * i + 2 * j for j in range(2) for i in bit_reversed(half // 2)]
+    order = [4 * i + 2 * j for j in (1, 0) for i in (4, 6, 5, 7, 2, 3, 1, 0)]
+    seq_order = [6, 7, 2, 3, 5, 1, 4, 0]
     same_core = [[i + c for i in order] for c in range(2)]
     partner = [(i, i ^ 1) for i in range(experts)]
 
@@ -285,25 +276,25 @@
         return lax.all_to_all(values, "expert", 0, 0, tiled=True, axis_index_groups=same_core)
 
     def exchange_seq(values):
-        return lax.all_to_all(values, "seq", 0, 0, tiled=True)
+        return lax.all_to_all(values, "seq", 0, 0, tiled=True, axis_index_groups=[seq_order])
 
     tokens_other, cotangent_other = swap(tokens), swap(cotangent)
     (message,) = call(copies_kernel, [((half, rows, width), BF16)], slot_keys)
-    keys, logits, columns = call(
+    keys, logits, columns, tokens_both = call(
         logit_kernel,
-        [((own, width), BF16), ((own, both), F32), ((2, both), F32)],
+        [((own, width), BF16), ((own, both), F32), ((2, both), F32), ((both, width), BF16)],
         exchange(message), tokens, tokens_other,
     )
     columns_other = swap(columns)
-    sums, stats = call(
+    sums, stats, cotangent_both = call(
         dispatch_kernel,
-        [((half, rows, width), BF16), ((half, rows, TAIL), BF16)],
-        logits, tokens, tokens_other,
+        [((half, rows, width), BF16), ((half, rows, TAIL), BF16), ((both, width), BF16)],
+        logits, tokens_both, cotangent, cotangent_other,
     )
     combine, message = call(
         combine_kernel,
         [((own, both), BF16), ((half, rows, long), BF16)],
-        logits, columns, columns_other, cotangent, cotangent_other, sums, stats,
+        logits, columns, columns_other, cotangent_both, sums, stats,
     )
     (message,) = call(merge_kernel, [((seq, rows, long), BF16)], exchange(message))
     parts, sums, stats, slot_in, out_grad, hidden, pre_grad = call(
@@ -326,18 +317,18 @@
     dots, columns = call(
         combine_dot_kernel,
         [((own, both), F32), ((2, both), F32)],
-        outs, cotangent, cotangent_other, combine,
+        outs, cotangent_both, combine,
     )
     columns_other = swap(columns)
     dispatch, term = call(
         pick_kernel,
         [((own, both), BF16), ((own, both), F32)],
-        outs, tokens, tokens_other, logits,
+        outs, tokens_both, logits,
     )
     message, logit_grad = call(
         key_kernel,
         [((half, rows, width), BF16), ((own, both), BF16)],
-        term, dots, combine, columns, columns_other, tokens, tokens_other,
+        term, dots, combine, columns, columns_other, tokens_both,
     )
     message = exchange(message)
     pack, weights = call(

time: 128 us -> 122 us (0.953)
  starting transfers between devices: 4.57 us -> 12.1 us
  blocking collectives: 98 us -> 90.6 us
  waiting for transfers between devices: 7.51 us -> 0.64 us
    all_to_all x1, starting transfers between devices: 3.53 us -> 11.1 us  [exchange(): lax.all_to_all(values, 'expert', 0, 0, tiled=True, axis_index_groups=same...]
    all_to_all x1, waiting for transfers between devices: 6.81 us -> 0.01 us  [exchange(): lax.all_to_all(values, 'expert', 0, 0, tiled=True, axis_index_groups=same...]
    all_to_all x3, blocking collectives: 68.1 us -> 62.2 us  [exchange(): lax.all_to_all(values, 'expert', 0, 0, tiled=True, axis_index_groups=same...]
    all_to_all x3, blocking collectives: 29.9 us -> 28.3 us  [exchange_seq(): lax.all_to_all(values, 'seq', 0, 0, tiled=True, axis_index_groups=[seq_or...]
  transfers between devices with their start and end apart: 6 -> 6, of which waited for: 3 -> 2; matrix products, arithmetic and copies ran while one was open for 5% -> 6% of each run, Pallas kernels for 2% -> 2%
where the time goes in v5:
time: 122 us; the launch traced here: 121 us
  blocking collectives  90.6 us (74%)
  starting transfers between devices  12.1 us (10%)
  Pallas kernels  7.99 us (7%)
  matrix products  7.01 us (6%)
  local copies, waits for them, and re-layouts  2.23 us (2%)
    all_to_all x3, blocking collectives, exchange(): lax.all_to_all(values, 'expert', 0, 0, tiled=True, axis_index_groups=same...  62.2 us
    all_to_all x3, blocking collectives, exchange_seq(): lax.all_to_all(values, 'seq', 0, 0, tiled=True, axis_index_groups=[seq_or...  28.3 us
    all_to_all x1, starting transfers between devices, exchange(): lax.all_to_all(values, 'expert', 0, 0, tiled=True, axis_index_groups=same...  11.1 us
    pallas_call x14, Pallas kernels, call(): pl.pallas_call(kernel, out_shape=[make(shape, dtype) for shape, dtype in...  7.99 us
    dot_general x4, matrix products, dot(): lax.dot_general(a, b, (((a_dim,), (b_dim,)), ((), ())), preferred_element...  7.01 us
  transfers between devices with their start and end apart: 6, of which 2 were waited for; matrix products, arithmetic and copies ran while one was open for 6% of the time, Pallas kernels for 2%

profile of v5, /device:TPU:2, one launch (start us, length us, event | category | flops | bytes accessed | tf_op | source)
XLA Modules:
  0.0 121.3 jit_solution(12855232087666560602)
XLA Ops:
  0.6 0.1 collective-permute-start
  0.7 0.5 collective-permute-start.2
  1.2 0.0 copy-start.4
  1.2 0.7 copy-done.4
  2.0 19.5 %all_to_all.35.message = bf16[16,2,4096]{2,1,0:T(2,128)(2,1)S(1)} all-to-all(bf16[16,2,4096]{2,1,0:T(2,128)(2,1)S(1)} %shard_map.92), channel_id=1, replica_groups={{18,26,22,30,10,14,6,2,16,24,20,28,8,12,4,0},{19,27,23,31,11,15,7,3,17,..., dimensions={0} | all-to-all | bytes 524288 | tf_op jit(solution)/shard_map/all_to_all | solution.py:276
  21.4 0.0 collective-permute-done.tokens_other
  21.4 0.0 copy-start.2
  21.4 1.2 %copy-done.2 = bf16[128,4096]{1,0:T(8,128)(2,1)S(1)} copy-done((bf16[128,4096]{1,0:T(8,128)(2,1)S(1)}, bf16[128,4096]{1,0:T(8,128)(2,1)}, u32[]{:S(2)}) %copy-start.2) | copy-done | bytes 1048600
  22.7 0.0 copy-start.3
  22.7 0.8 shard_map.93
  23.5 0.1 collective-permute-start.1
  23.6 0.0 collective-permute-done.2.cotangent_other
  23.6 0.3 copy-done.3
  23.9 0.6 shard_map.94
  24.5 0.2 collective-permute-done.1.columns_other
  24.7 0.0 copy-start
  24.7 0.0 copy-start.1
  24.7 0.5 shard_map.95
  25.2 22.5 %all_to_all.36.message = bf16[16,2,8448]{2,1,0:T(2,128)(2,1)S(1)} all-to-all(bf16[16,2,8448]{2,1,0:T(2,128)(2,1)S(1)} %get-tuple-element.43), channel_id=1, replica_groups={{18,26,22,30,10,14,6,2,16,24,20,28,8,12,4,0},{19,27,23,31,11,15,7,3,17,..., dimensions={0} | all-to-all | bytes 1081344 | tf_op jit(solution)/shard_map/all_to_all | solution.py:276
  47.7 0.3 shard_map.96
  48.0 10.0 %all_to_all.37.message = bf16[8,2,8448]{2,1,0:T(2,128)(2,1)S(1)} all-to-all(bf16[8,2,8448]{2,1,0:T(2,128)(2,1)S(1)} %shard_map.96), channel_id=1, replica_groups={{192,224,64,96,160,32,128,0},{193,225,65,97,161,33,129,1},{194,226,66,9..., dimensions={0} | all-to-all | bytes 540672 | tf_op jit(solution)/shard_map/all_to_all | solution.py:279
  58.0 0.0 copy-done
  58.0 0.0 copy-done.1
  58.0 2.1 %shard_map.97 = (bf16[8,2,8192]{2,1,0:T(2,128)(2,1)S(1)}, f32[2,4096]{1,0:T(2,128)S(1)}, f32[2,128]{1,0:T(2,128)S(1)}, bf16[2,4096]{1,0:T(2,128)(2,1)S(1)}, bf16...) custom-call(bf16[8,2,8448]{2,1,0:T(2,128)(2,1)S(1)} %all_to_all.37.message, ...), custom_call_target="tpu_custom_call" | custom-call | tf_op jit(solution)/shard_map/pallas_call | solution.py:248
  60.1 9.4 %all_to_all.38.parts = bf16[8,2,8192]{2,1,0:T(2,128)(2,1)S(1)} all-to-all(bf16[8,2,8192]{2,1,0:T(2,128)(2,1)S(1)} %get-tuple-element.44), channel_id=1, replica_groups={{192,224,64,96,160,32,128,0},{193,225,65,97,161,33,129,1},{194,226,66,9..., dimensions={0} | all-to-all | bytes 524288 | tf_op jit(solution)/shard_map/all_to_all | solution.py:279
  69.5 0.2 shard_map.98
  69.7 20.3 %all_to_all.39.outs = bf16[16,2,8448]{2,1,0:T(2,128)(2,1)S(1)} all-to-all(bf16[16,2,8448]{2,1,0:T(2,128)(2,1)S(1)} %shard_map.98), channel_id=1, replica_groups={{18,26,22,30,10,14,6,2,16,24,20,28,8,12,4,0},{19,27,23,31,11,15,7,3,17,..., dimensions={0} | all-to-all | bytes 1081344 | tf_op jit(solution)/shard_map/all_to_all | solution.py:276
  90.0 0.7 shard_map.100
  90.7 0.1 collective-permute-start.3
  90.8 0.7 shard_map.99
  91.6 0.4 collective-permute-done.3.columns_other
  92.0 1.2 shard_map.101
  93.2 0.1 shard_map.102
  93.2 0.3 collective-permute-start.4
  93.5 11.1 %all-to-all-start.5 = ((bf16[16,2,4096]{2,1,0:T(2,128)(2,1)}), bf16[16,2,4096]{2,1,0:T(2,128)(2,1)S(1)}, u32[]{:S(2)}, u32[]{:S(2)}) async-start(bf16[16,2,4096]{2,1,0:T(2,128)(2,1)} %get-tuple-element.64), calls=%async_computation.5 | async-start | bytes 524288 | tf_op jit(solution)/shard_map/all_to_all | solution.py:276
  104.6 0.0 collective-permute-done.4.pack_other
  104.6 0.1 shard_map.103
  104.7 2.1 %fusion.refs_2_ = bf16[1,4096,256]{2,1,0:T(8,128)(2,1)} fusion(bf16[2,4096]{1,0:T(2,128)(2,1)S(1)} %get-tuple-element.65, bf16[2,256]{1,0:T(2,128)(2,1)S(1)} %get-tuple-element.66), kind=kOutput, calls=%fused_computation.2 | convolution fusion | flops 5242880 | bytes 2114560 | tf_op jit(solution)/shard_map/dot_general | solution.py:18
  106.8 2.1 %fusion.1.refs_3_ = bf16[1,256,4096]{2,1,0:T(8,128)(2,1)} fusion(bf16[2,256]{1,0:T(2,128)(2,1)S(1)} %get-tuple-element.67, bf16[2,4096]{1,0:T(2,128)(2,1)S(1)} %get-tuple-element.68), kind=kOutput, calls=%fused_computation.3 | convolution fusion | flops 5242880 | bytes 2114560 | tf_op jit(solution)/shard_map/dot_general | solution.py:18
  108.9 1.4 %convolution_convert_fusion.3.refs_0_ = bf16[128,4096]{1,0:T(8,128)(2,1)} fusion(bf16[64,128]{1,0:T(8,128)(2,1)S(1)} %get-tuple-element.60, bf16[64,4096]{1,0:T(8,128)(2,1)S(1)} %get-tuple-element.61), kind=kOutput, calls=%fused_computation.5 | convolution fusion | flops 67633152 | bytes 1589248 | tf_op jit(solution)/shard_map/dot_general | solution.py:18
  110.3 1.4 %convolution_convert_fusion.2.refs_1_ = bf16[128,4096]{1,0:T(8,128)(2,1)} fusion(bf16[128,128]{1,0:T(8,128)(2,1)S(1)} %get-tuple-element.62, bf16[128,4096]{1,0:T(8,128)(2,1)S(1)} %get-tuple-element.63), kind=kOutput, calls=%fused_computation.4 | convolution fusion | flops 134742016 | bytes 2129920 | tf_op jit(solution)/shard_map/dot_general | solution.py:18
  111.8 0.0 all-to-all-done.5.message
  111.8 0.1 shard_map.104
  111.8 8.9 %all_to_all.40.message = bf16[8,2,4096]{2,1,0:T(2,128)(2,1)S(1)} all-to-all(bf16[8,2,4096]{2,1,0:T(2,128)(2,1)S(1)} %shard_map.104), channel_id=1, replica_groups={{192,224,64,96,160,32,128,0},{193,225,65,97,161,33,129,1},{194,226,66,9..., dimensions={0} | all-to-all | bytes 262144 | tf_op jit(solution)/shard_map/all_to_all | solution.py:279
  120.7 0.6 shard_map.105
  (1 shorter events, 0.0 us)
Async XLA Ops:
  0.6 20.8 %collective-permute-start = (bf16[128,4096]{1,0:T(8,128)(2,1)}, bf16[128,4096]{1,0:T(8,128)(2,1)S(1)}, u32[]{:S(2)}, u32[]{:S(2)}) collective-permute-start(bf16[128,4096]{1,0:T(8,128)(2,1)} %tokens.1), channel_id=1, source_target_pairs={{0,1},{1,0},{2,3},{3,2},{4,5},{5,4},{6,7},{7,6},{8,9},{9,8},{10,11... | collective-permute-start | bytes 3145736 | tf_op jit(solution)/shard_map/ppermute | solution.py:273
  0.7 22.9 %collective-permute-start.2 = (bf16[128,4096]{1,0:T(8,128)(2,1)}, bf16[128,4096]{1,0:T(8,128)(2,1)S(1)}, u32[]{:S(2)}, u32[]{:S(2)}) collective-permute-start(bf16[128,4096]{1,0:T(8,128)(2,1)} %cotangent.1), channel_id=1, source_target_pairs={{0,1},{1,0},{2,3},{3,2},{4,5},{5,4},{6,7},{7,6},{8,9},{9,8},{10,11... | collective-permute-start | bytes 3145736 | tf_op jit(solution)/shard_map/ppermute | solution.py:273
  1.2 0.7 copy-start.4
  21.4 1.2 %copy-start.2 = (bf16[128,4096]{1,0:T(8,128)(2,1)S(1)}, bf16[128,4096]{1,0:T(8,128)(2,1)}, u32[]{:S(2)}) copy-start(bf16[128,4096]{1,0:T(8,128)(2,1)} %tokens.1) | copy-start | bytes 3145732
  22.7 1.2 %copy-start.3 = (bf16[128,4096]{1,0:T(8,128)(2,1)S(1)}, bf16[128,4096]{1,0:T(8,128)(2,1)}, u32[]{:S(2)}) copy-start(bf16[128,4096]{1,0:T(8,128)(2,1)} %cotangent.1) | copy-start | bytes 3145732
  23.5 1.2 %collective-permute-start.1 = (f32[2,256]{1,0:T(2,128)S(1)}, f32[2,256]{1,0:T(2,128)S(1)}, u32[]{:S(2)}, u32[]{:S(2)}) collective-permute-start(f32[2,256]{1,0:T(2,128)S(1)} %get-tuple-element.38.columns), channel_id=1, source_target_pairs={{0,1},{1,0},{2,3},{3,2},{4,5},{5,4},{6,7},{7,6},{8,9},{9,8},{10,11... | collective-permute-start | bytes 6152 | tf_op jit(solution)/shard_map/ppermute | solution.py:273
  24.7 33.3 %copy-start = (bf16[1,4096,256]{2,1,0:T(8,128)(2,1)S(1)}, bf16[1,4096,256]{2,1,0:T(8,128)(2,1)}, u32[]{:S(2)}) copy-start(bf16[1,4096,256]{2,1,0:T(8,128)(2,1)} %param.7) | copy-start | bytes 6291460
  24.7 33.3 %copy-start.1 = (bf16[1,256,4096]{2,1,0:T(8,128)(2,1)S(1)}, bf16[1,256,4096]{2,1,0:T(8,128)(2,1)}, u32[]{:S(2)}) copy-start(bf16[1,256,4096]{2,1,0:T(8,128)(2,1)} %param.8) | copy-start | bytes 6291460
  90.7 1.2 %collective-permute-start.3 = (f32[2,256]{1,0:T(2,128)S(1)}, f32[2,256]{1,0:T(2,128)S(1)}, u32[]{:S(2)}, u32[]{:S(2)}) collective-permute-start(f32[2,256]{1,0:T(2,128)S(1)} %get-tuple-element.52.columns), channel_id=1, source_target_pairs={{0,1},{1,0},{2,3},{3,2},{4,5},{5,4},{6,7},{7,6},{8,9},{9,8},{10,11... | collective-permute-start | bytes 6152 | tf_op jit(solution)/shard_map/ppermute | solution.py:273
  93.2 11.4 %collective-permute-start.4 = (bf16[32,12672]{1,0:T(8,128)(2,1)S(1)}, bf16[32,12672]{1,0:T(8,128)(2,1)S(1)}, u32[]{:S(2)}, u32[]{:S(2)}) collective-permute-start(bf16[32,12672]{1,0:T(8,128)(2,1)S(1)} %get-tuple-element.54.pack), channel_id=1, source_target_pairs={{0,1},{1,0},{2,3},{3,2},{4,5},{5,4},{6,7},{7,6},{8,9},{9,8},{10,11... | collective-permute-start | bytes 2433032 | tf_op jit(solution)/shard_map/ppermute | solution.py:273
  93.5 18.3 %all-to-all-start.5 = ((bf16[16,2,4096]{2,1,0:T(2,128)(2,1)}), bf16[16,2,4096]{2,1,0:T(2,128)(2,1)S(1)}, u32[]{:S(2)}, u32[]{:S(2)}) async-start(bf16[16,2,4096]{2,1,0:T(2,128)(2,1)} %get-tuple-element.64), calls=%async_computation.5 | async-start | bytes 524288 | tf_op jit(solution)/shard_map/all_to_all | solution.py:276

commit v6 on v5

--- a/solution.py
+++ b/solution.py
@@ -9,7 +9,7 @@
 
 F32 = jnp.float32
 BF16 = jnp.bfloat16
-TAIL = 256
+TAIL = 128
 ROOT = math.sqrt(2.0 / math.pi)
 CUBE = 0.044715
 
@@ -264,7 +264,7 @@
     own = half * rows
     both = 2 * count
     long = 2 * width + TAIL
-    order = [4 * i + 2 * j for j in (1, 0) for i in (4, 6, 5, 7, 2, 3, 1, 0)]
+    order = [4 * i + 2 * j for j in (1, 0) for i in (4, 6, 2, 5, 7, 3, 1, 0)]
     seq_order = [6, 7, 2, 3, 5, 1, 4, 0]
     same_core = [[i + c for i in order] for c in range(2)]
     partner = [(i, i ^ 1) for i in range(experts)]

time: 122 us -> 122 us (level)
  no operation moved by 1% of the time
where the time goes in v6:
time: 122 us; the launch traced here: 120 us
  blocking collectives  90.4 us (74%)
  starting transfers between devices  11.5 us (9%)
  Pallas kernels  7.98 us (7%)
  matrix products  7.02 us (6%)
  local copies, waits for them, and re-layouts  2.24 us (2%)
    all_to_all x3, blocking collectives, exchange(): lax.all_to_all(values, 'expert', 0, 0, tiled=True, axis_index_groups=same...  62.1 us
    all_to_all x3, blocking collectives, exchange_seq(): lax.all_to_all(values, 'seq', 0, 0, tiled=True, axis_index_groups=[seq_or...  28.3 us
    all_to_all x1, starting transfers between devices, exchange(): lax.all_to_all(values, 'expert', 0, 0, tiled=True, axis_index_groups=same...  10.4 us
    pallas_call x14, Pallas kernels, call(): pl.pallas_call(kernel, out_shape=[make(shape, dtype) for shape, dtype in...  7.98 us
    dot_general x4, matrix products, dot(): lax.dot_general(a, b, (((a_dim,), (b_dim,)), ((), ())), preferred_element...  7.02 us
  transfers between devices with their start and end apart: 6, of which 2 were waited for; matrix products, arithmetic and copies ran while one was open for 6% of the time, Pallas kernels for 2%

profile of v6, /device:TPU:2, one launch (start us, length us, event | category | flops | bytes accessed | tf_op | source)
XLA Modules:
  0.0 120.5 jit_solution(541636041711980243)
XLA Ops:
  0.6 0.1 collective-permute-start
  0.7 0.5 collective-permute-start.2
  1.2 0.0 copy-start.4
  1.2 0.7 copy-done.4
  2.0 19.4 %all_to_all.35.message = bf16[16,2,4096]{2,1,0:T(2,128)(2,1)S(1)} all-to-all(bf16[16,2,4096]{2,1,0:T(2,128)(2,1)S(1)} %shard_map.92), channel_id=1, replica_groups={{18,26,10,22,30,14,6,2,16,24,8,20,28,12,4,0},{19,27,11,23,31,15,7,3,17,..., dimensions={0} | all-to-all | bytes 524288 | tf_op jit(solution)/shard_map/all_to_all | solution.py:276
  21.4 0.0 collective-permute-done.tokens_other
  21.4 0.0 copy-start.2
  21.4 1.2 %copy-done.2 = bf16[128,4096]{1,0:T(8,128)(2,1)S(1)} copy-done((bf16[128,4096]{1,0:T(8,128)(2,1)S(1)}, bf16[128,4096]{1,0:T(8,128)(2,1)}, u32[]{:S(2)}) %copy-start.2) | copy-done | bytes 1048600
  22.6 0.0 copy-start.3
  22.6 0.8 shard_map.93
  23.5 0.1 collective-permute-start.1
  23.6 0.0 collective-permute-done.2.cotangent_other
  23.6 0.3 copy-done.3
  23.9 0.6 shard_map.94
  24.5 0.2 collective-permute-done.1.columns_other
  24.7 0.0 copy-start
  24.7 0.0 copy-start.1
  24.7 0.5 shard_map.95
  25.2 22.3 %all_to_all.36.message = bf16[16,2,8320]{2,1,0:T(2,128)(2,1)S(1)} all-to-all(bf16[16,2,8320]{2,1,0:T(2,128)(2,1)S(1)} %get-tuple-element.43), channel_id=1, replica_groups={{18,26,10,22,30,14,6,2,16,24,8,20,28,12,4,0},{19,27,11,23,31,15,7,3,17,..., dimensions={0} | all-to-all | bytes 1064960 | tf_op jit(solution)/shard_map/all_to_all | solution.py:276
  47.5 0.3 shard_map.96
  47.8 10.0 %all_to_all.37.message = bf16[8,2,8320]{2,1,0:T(2,128)(2,1)S(1)} all-to-all(bf16[8,2,8320]{2,1,0:T(2,128)(2,1)S(1)} %shard_map.96), channel_id=1, replica_groups={{192,224,64,96,160,32,128,0},{193,225,65,97,161,33,129,1},{194,226,66,9..., dimensions={0} | all-to-all | bytes 532480 | tf_op jit(solution)/shard_map/all_to_all | solution.py:279
  57.8 0.0 copy-done
  57.8 0.0 copy-done.1
  57.8 2.1 %shard_map.97 = (bf16[8,2,8192]{2,1,0:T(2,128)(2,1)S(1)}, f32[2,4096]{1,0:T(2,128)S(1)}, f32[2,128]{1,0:T(2,128)S(1)}, bf16[2,4096]{1,0:T(2,128)(2,1)S(1)}, bf16...) custom-call(bf16[8,2,8320]{2,1,0:T(2,128)(2,1)S(1)} %all_to_all.37.message, ...), custom_call_target="tpu_custom_call" | custom-call | tf_op jit(solution)/shard_map/pallas_call | solution.py:248
  59.9 9.5 %all_to_all.38.parts = bf16[8,2,8192]{2,1,0:T(2,128)(2,1)S(1)} all-to-all(bf16[8,2,8192]{2,1,0:T(2,128)(2,1)S(1)} %get-tuple-element.44), channel_id=1, replica_groups={{192,224,64,96,160,32,128,0},{193,225,65,97,161,33,129,1},{194,226,66,9..., dimensions={0} | all-to-all | bytes 524288 | tf_op jit(solution)/shard_map/all_to_all | solution.py:279
  69.3 0.2 shard_map.98
  69.5 20.3 %all_to_all.39.outs = bf16[16,2,8320]{2,1,0:T(2,128)(2,1)S(1)} all-to-all(bf16[16,2,8320]{2,1,0:T(2,128)(2,1)S(1)} %shard_map.98), channel_id=1, replica_groups={{18,26,10,22,30,14,6,2,16,24,8,20,28,12,4,0},{19,27,11,23,31,15,7,3,17,..., dimensions={0} | all-to-all | bytes 1064960 | tf_op jit(solution)/shard_map/all_to_all | solution.py:276
  89.8 0.7 shard_map.100
  90.6 0.1 collective-permute-start.3
  90.7 0.7 shard_map.99
  91.4 0.4 collective-permute-done.3.columns_other
  91.8 1.2 shard_map.101
  93.0 0.1 shard_map.102
  93.1 0.3 collective-permute-start.4
  93.3 10.4 %all-to-all-start.5 = ((bf16[16,2,4096]{2,1,0:T(2,128)(2,1)}), bf16[16,2,4096]{2,1,0:T(2,128)(2,1)S(1)}, u32[]{:S(2)}, u32[]{:S(2)}) async-start(bf16[16,2,4096]{2,1,0:T(2,128)(2,1)} %get-tuple-element.64), calls=%async_computation.5 | async-start | bytes 524288 | tf_op jit(solution)/shard_map/all_to_all | solution.py:276
  103.8 0.0 collective-permute-done.4.pack_other
  103.8 0.1 shard_map.103
  103.9 2.1 %fusion.refs_2_ = bf16[1,4096,256]{2,1,0:T(8,128)(2,1)} fusion(bf16[2,4096]{1,0:T(2,128)(2,1)S(1)} %get-tuple-element.65, bf16[2,256]{1,0:T(2,128)(2,1)S(1)} %get-tuple-element.66), kind=kOutput, calls=%fused_computation.2 | convolution fusion | flops 5242880 | bytes 2114560 | tf_op jit(solution)/shard_map/dot_general | solution.py:18
  106.0 2.1 %fusion.1.refs_3_ = bf16[1,256,4096]{2,1,0:T(8,128)(2,1)} fusion(bf16[2,256]{1,0:T(2,128)(2,1)S(1)} %get-tuple-element.67, bf16[2,4096]{1,0:T(2,128)(2,1)S(1)} %get-tuple-element.68), kind=kOutput, calls=%fused_computation.3 | convolution fusion | flops 5242880 | bytes 2114560 | tf_op jit(solution)/shard_map/dot_general | solution.py:18
  108.1 1.4 %convolution_convert_fusion.3.refs_0_ = bf16[128,4096]{1,0:T(8,128)(2,1)} fusion(bf16[64,128]{1,0:T(8,128)(2,1)S(1)} %get-tuple-element.60, bf16[64,4096]{1,0:T(8,128)(2,1)S(1)} %get-tuple-element.61), kind=kOutput, calls=%fused_computation.5 | convolution fusion | flops 67633152 | bytes 1589248 | tf_op jit(solution)/shard_map/dot_general | solution.py:18
  109.5 1.4 %convolution_convert_fusion.2.refs_1_ = bf16[128,4096]{1,0:T(8,128)(2,1)} fusion(bf16[128,128]{1,0:T(8,128)(2,1)S(1)} %get-tuple-element.62, bf16[128,4096]{1,0:T(8,128)(2,1)S(1)} %get-tuple-element.63), kind=kOutput, calls=%fused_computation.4 | convolution fusion | flops 134742016 | bytes 2129920 | tf_op jit(solution)/shard_map/dot_general | solution.py:18
  110.9 0.0 all-to-all-done.5.message
  110.9 0.1 shard_map.104
  111.0 8.8 %all_to_all.40.message = bf16[8,2,4096]{2,1,0:T(2,128)(2,1)S(1)} all-to-all(bf16[8,2,4096]{2,1,0:T(2,128)(2,1)S(1)} %shard_map.104), channel_id=1, replica_groups={{192,224,64,96,160,32,128,0},{193,225,65,97,161,33,129,1},{194,226,66,9..., dimensions={0} | all-to-all | bytes 262144 | tf_op jit(solution)/shard_map/all_to_all | solution.py:279
  119.8 0.6 shard_map.105
  (1 shorter events, 0.0 us)
Async XLA Ops:
  0.6 20.8 %collective-permute-start = (bf16[128,4096]{1,0:T(8,128)(2,1)}, bf16[128,4096]{1,0:T(8,128)(2,1)S(1)}, u32[]{:S(2)}, u32[]{:S(2)}) collective-permute-start(bf16[128,4096]{1,0:T(8,128)(2,1)} %tokens.1), channel_id=1, source_target_pairs={{0,1},{1,0},{2,3},{3,2},{4,5},{5,4},{6,7},{7,6},{8,9},{9,8},{10,11... | collective-permute-start | bytes 3145736 | tf_op jit(solution)/shard_map/ppermute | solution.py:273
  0.7 22.8 %collective-permute-start.2 = (bf16[128,4096]{1,0:T(8,128)(2,1)}, bf16[128,4096]{1,0:T(8,128)(2,1)S(1)}, u32[]{:S(2)}, u32[]{:S(2)}) collective-permute-start(bf16[128,4096]{1,0:T(8,128)(2,1)} %cotangent.1), channel_id=1, source_target_pairs={{0,1},{1,0},{2,3},{3,2},{4,5},{5,4},{6,7},{7,6},{8,9},{9,8},{10,11... | collective-permute-start | bytes 3145736 | tf_op jit(solution)/shard_map/ppermute | solution.py:273
  1.2 0.7 copy-start.4
  21.4 1.2 %copy-start.2 = (bf16[128,4096]{1,0:T(8,128)(2,1)S(1)}, bf16[128,4096]{1,0:T(8,128)(2,1)}, u32[]{:S(2)}) copy-start(bf16[128,4096]{1,0:T(8,128)(2,1)} %tokens.1) | copy-start | bytes 3145732
  22.6 1.2 %copy-start.3 = (bf16[128,4096]{1,0:T(8,128)(2,1)S(1)}, bf16[128,4096]{1,0:T(8,128)(2,1)}, u32[]{:S(2)}) copy-start(bf16[128,4096]{1,0:T(8,128)(2,1)} %cotangent.1) | copy-start | bytes 3145732
  23.5 1.2 %collective-permute-start.1 = (f32[2,256]{1,0:T(2,128)S(1)}, f32[2,256]{1,0:T(2,128)S(1)}, u32[]{:S(2)}, u32[]{:S(2)}) collective-permute-start(f32[2,256]{1,0:T(2,128)S(1)} %get-tuple-element.38.columns), channel_id=1, source_target_pairs={{0,1},{1,0},{2,3},{3,2},{4,5},{5,4},{6,7},{7,6},{8,9},{9,8},{10,11... | collective-permute-start | bytes 6152 | tf_op jit(solution)/shard_map/ppermute | solution.py:273
  24.7 33.1 %copy-start = (bf16[1,4096,256]{2,1,0:T(8,128)(2,1)S(1)}, bf16[1,4096,256]{2,1,0:T(8,128)(2,1)}, u32[]{:S(2)}) copy-start(bf16[1,4096,256]{2,1,0:T(8,128)(2,1)} %param.7) | copy-start | bytes 6291460
  24.7 33.1 %copy-start.1 = (bf16[1,256,4096]{2,1,0:T(8,128)(2,1)S(1)}, bf16[1,256,4096]{2,1,0:T(8,128)(2,1)}, u32[]{:S(2)}) copy-start(bf16[1,256,4096]{2,1,0:T(8,128)(2,1)} %param.8) | copy-start | bytes 6291460
  90.6 1.2 %collective-permute-start.3 = (f32[2,256]{1,0:T(2,128)S(1)}, f32[2,256]{1,0:T(2,128)S(1)}, u32[]{:S(2)}, u32[]{:S(2)}) collective-permute-start(f32[2,256]{1,0:T(2,128)S(1)} %get-tuple-element.52.columns), channel_id=1, source_target_pairs={{0,1},{1,0},{2,3},{3,2},{4,5},{5,4},{6,7},{7,6},{8,9},{9,8},{10,11... | collective-permute-start | bytes 6152 | tf_op jit(solution)/shard_map/ppermute | solution.py:273
  93.1 10.7 %collective-permute-start.4 = (bf16[32,12672]{1,0:T(8,128)(2,1)S(1)}, bf16[32,12672]{1,0:T(8,128)(2,1)S(1)}, u32[]{:S(2)}, u32[]{:S(2)}) collective-permute-start(bf16[32,12672]{1,0:T(8,128)(2,1)S(1)} %get-tuple-element.54.pack), channel_id=1, source_target_pairs={{0,1},{1,0},{2,3},{3,2},{4,5},{5,4},{6,7},{7,6},{8,9},{9,8},{10,11... | collective-permute-start | bytes 2433032 | tf_op jit(solution)/shard_map/ppermute | solution.py:273
  93.3 17.6 %all-to-all-start.5 = ((bf16[16,2,4096]{2,1,0:T(2,128)(2,1)}), bf16[16,2,4096]{2,1,0:T(2,128)(2,1)S(1)}, u32[]{:S(2)}, u32[]{:S(2)}) async-start(bf16[16,2,4096]{2,1,0:T(2,128)(2,1)} %get-tuple-element.64), calls=%async_computation.5 | async-start | bytes 524288 | tf_op jit(solution)/shard_map/all_to_all | solution.py:276

commit v7 on v6

--- a/solution.py
+++ b/solution.py
@@ -254,6 +254,39 @@
     )(*args)
 
 
+def weight_kernel(slot_in, pre_grad, hidden, out_grad, w_in_grad, w_out_grad):
+    w_in_grad[0] = dot(slot_in[...], pre_grad[...], 0, 0).astype(BF16)
+    w_out_grad[0] = dot(hidden[...], out_grad[...], 0, 0).astype(BF16)
+
+
+def weight_grads(slot_in, pre_grad, hidden, out_grad):
+    rows, width = slot_in.shape
+    units = hidden.shape[1]
+    steps = 4
+    return pl.pallas_call(
+        weight_kernel,
+        grid=(steps,),
+        out_shape=[
+            jax.ShapeDtypeStruct((1, width, units), BF16),
+            jax.ShapeDtypeStruct((1, units, width), BF16),
+        ],
+        in_specs=[
+            pl.BlockSpec((rows, width // steps), lambda i: (0, i)),
+            pl.BlockSpec((rows, units), lambda i: (0, 0)),
+            pl.BlockSpec((rows, units), lambda i: (0, 0)),
+            pl.BlockSpec((rows, width // steps), lambda i: (0, i)),
+        ],
+        out_specs=[
+            pl.BlockSpec((1, width // steps, units), lambda i: (0, i, 0)),
+            pl.BlockSpec((1, units, width // steps), lambda i: (0, 0, i)),
+        ],
+        compiler_params=pltpu.CompilerParams(vmem_limit_bytes=16 * 1024 * 1024),
+        cost_estimate=pl.CostEstimate(
+            flops=4 * rows * width * units, bytes_accessed=4 * width * units, transcendentals=0
+        ),
+    )(slot_in, pre_grad, hidden, out_grad)
+
+
 def body(tokens, slot_keys, w_in, w_out, cotangent):
     count, width = tokens.shape
     hidden_units = w_in.shape[2]
@@ -350,8 +383,7 @@
     )
     layer_out = dot(combine, slot_out, 0, 0).astype(BF16)
     token_grad = dot(rest_weights, rest, 0, 0).astype(BF16)
-    w_out_grad = dot(hidden, out_grad, 0, 0).astype(BF16)[None]
-    w_in_grad = dot(slot_in, pre_grad, 0, 0).astype(BF16)[None]
+    w_in_grad, w_out_grad = weight_grads(slot_in, pre_grad, hidden, out_grad)
     results = (layer_out, token_grad, w_in_grad, w_out_grad)
     (message,) = call(
         key_merge_kernel, [((seq, rows, width), BF16)], message, *results, far=(1, 2, 3, 4)

time: 122 us -> 122 us (level)
  matrix products: 7.02 us -> 2.86 us
  Pallas kernels: 7.98 us -> 11.3 us
    dot_general x4 -> x2, matrix products: 7.02 us -> 2.86 us  [dot(): lax.dot_general(a, b, (((a_dim,), (b_dim,)), ((), ())), preferred_element...]
    pallas_call x0 -> x1, Pallas kernels: none -> 3.36 us  [weight_grads(): pl.pallas_call(weight_kernel, grid=(steps,), out_shape=[jax.ShapeDtypeStr...]
  transfers between devices with their start and end apart: 6 -> 6, of which waited for: 2 -> 3; matrix products, arithmetic and copies ran while one was open for 6% -> 2% of each run, Pallas kernels for 2% -> 5%
where the time goes in v7:
time: 122 us; the launch traced here: 120 us
  blocking collectives  90.4 us (74%)
  starting transfers between devices  11.5 us (9%)
  Pallas kernels  11.3 us (9%)
  matrix products  2.86 us (2%)
  local copies, waits for them, and re-layouts  2.24 us (2%)
  waiting for transfers between devices  1.31 us (1%)
    all_to_all x3, blocking collectives, exchange(): lax.all_to_all(values, 'expert', 0, 0, tiled=True, axis_index_groups=same...  62.1 us
    all_to_all x3, blocking collectives, exchange_seq(): lax.all_to_all(values, 'seq', 0, 0, tiled=True, axis_index_groups=[seq_or...  28.3 us
    all_to_all x1, starting transfers between devices, exchange(): lax.all_to_all(values, 'expert', 0, 0, tiled=True, axis_index_groups=same...  10.4 us
    pallas_call x14, Pallas kernels, call(): pl.pallas_call(kernel, out_shape=[make(shape, dtype) for shape, dtype in...  7.98 us
    pallas_call x1, Pallas kernels, weight_grads(): pl.pallas_call(weight_kernel, grid=(steps,), out_shape=[jax.ShapeDtypeStr...  3.36 us
    dot_general x2, matrix products, dot(): lax.dot_general(a, b, (((a_dim,), (b_dim,)), ((), ())), preferred_element...  2.86 us
  transfers between devices with their start and end apart: 6, of which 3 were waited for; matrix products, arithmetic and copies ran while one was open for 2% of the time, Pallas kernels for 5%

profile of v7, /device:TPU:2, one launch (start us, length us, event | category | flops | bytes accessed | tf_op | source)
XLA Modules:
  0.0 120.3 jit_solution(4520677152868286003)
XLA Ops:
  0.6 0.1 collective-permute-start
  0.7 0.5 collective-permute-start.2
  1.2 0.0 copy-start.4
  1.2 0.7 copy-done.4
  2.0 19.4 %all_to_all.35.message = bf16[16,2,4096]{2,1,0:T(2,128)(2,1)S(1)} all-to-all(bf16[16,2,4096]{2,1,0:T(2,128)(2,1)S(1)} %shard_map.92), channel_id=1, replica_groups={{18,26,10,22,30,14,6,2,16,24,8,20,28,12,4,0},{19,27,11,23,31,15,7,3,17,..., dimensions={0} | all-to-all | bytes 524288 | tf_op jit(solution)/shard_map/all_to_all | solution.py:309
  21.4 0.0 collective-permute-done.tokens_other
  21.4 0.0 copy-start.2
  21.4 1.2 %copy-done.2 = bf16[128,4096]{1,0:T(8,128)(2,1)S(1)} copy-done((bf16[128,4096]{1,0:T(8,128)(2,1)S(1)}, bf16[128,4096]{1,0:T(8,128)(2,1)}, u32[]{:S(2)}) %copy-start.2) | copy-done | bytes 1048600
  22.6 0.0 copy-start.3
  22.6 0.8 shard_map.93
  23.5 0.1 collective-permute-start.1
  23.6 0.0 collective-permute-done.2.cotangent_other
  23.6 0.3 copy-done.3
  23.9 0.6 shard_map.94
  24.5 0.2 collective-permute-done.1.columns_other
  24.7 0.0 copy-start
  24.7 0.0 copy-start.1
  24.7 0.5 shard_map.95
  25.2 22.3 %all_to_all.36.message = bf16[16,2,8320]{2,1,0:T(2,128)(2,1)S(1)} all-to-all(bf16[16,2,8320]{2,1,0:T(2,128)(2,1)S(1)} %get-tuple-element.45), channel_id=1, replica_groups={{18,26,10,22,30,14,6,2,16,24,8,20,28,12,4,0},{19,27,11,23,31,15,7,3,17,..., dimensions={0} | all-to-all | bytes 1064960 | tf_op jit(solution)/shard_map/all_to_all | solution.py:309
  47.5 0.3 shard_map.96
  47.8 10.0 %all_to_all.37.message = bf16[8,2,8320]{2,1,0:T(2,128)(2,1)S(1)} all-to-all(bf16[8,2,8320]{2,1,0:T(2,128)(2,1)S(1)} %shard_map.96), channel_id=1, replica_groups={{192,224,64,96,160,32,128,0},{193,225,65,97,161,33,129,1},{194,226,66,9..., dimensions={0} | all-to-all | bytes 532480 | tf_op jit(solution)/shard_map/all_to_all | solution.py:312
  57.8 0.0 copy-done
  57.8 0.0 copy-done.1
  57.8 2.1 %shard_map.97 = (bf16[8,2,8192]{2,1,0:T(2,128)(2,1)S(1)}, f32[2,4096]{1,0:T(2,128)S(1)}, f32[2,128]{1,0:T(2,128)S(1)}, bf16[2,4096]{1,0:T(2,128)(2,1)S(1)}, bf16...) custom-call(bf16[8,2,8320]{2,1,0:T(2,128)(2,1)S(1)} %all_to_all.37.message, ...), custom_call_target="tpu_custom_call" | custom-call | tf_op jit(solution)/shard_map/pallas_call | solution.py:248
  59.9 9.5 %all_to_all.38.parts = bf16[8,2,8192]{2,1,0:T(2,128)(2,1)S(1)} all-to-all(bf16[8,2,8192]{2,1,0:T(2,128)(2,1)S(1)} %get-tuple-element.46), channel_id=1, replica_groups={{192,224,64,96,160,32,128,0},{193,225,65,97,161,33,129,1},{194,226,66,9..., dimensions={0} | all-to-all | bytes 524288 | tf_op jit(solution)/shard_map/all_to_all | solution.py:312
  69.3 0.2 shard_map.98
  69.5 20.3 %all_to_all.39.outs = bf16[16,2,8320]{2,1,0:T(2,128)(2,1)S(1)} all-to-all(bf16[16,2,8320]{2,1,0:T(2,128)(2,1)S(1)} %shard_map.98), channel_id=1, replica_groups={{18,26,10,22,30,14,6,2,16,24,8,20,28,12,4,0},{19,27,11,23,31,15,7,3,17,..., dimensions={0} | all-to-all | bytes 1064960 | tf_op jit(solution)/shard_map/all_to_all | solution.py:309
  89.8 0.7 shard_map.100
  90.6 0.1 collective-permute-start.3
  90.7 0.7 shard_map.99
  91.4 0.4 collective-permute-done.3.columns_other
  91.8 1.2 shard_map.101
  93.0 0.1 shard_map.102
  93.1 0.3 collective-permute-start.4
  93.3 10.4 %all-to-all-start.5 = ((bf16[16,2,4096]{2,1,0:T(2,128)(2,1)}), bf16[16,2,4096]{2,1,0:T(2,128)(2,1)S(1)}, u32[]{:S(2)}, u32[]{:S(2)}) async-start(bf16[16,2,4096]{2,1,0:T(2,128)(2,1)} %get-tuple-element.66), calls=%async_computation.5 | async-start | bytes 524288 | tf_op jit(solution)/shard_map/all_to_all | solution.py:309
  103.8 0.0 collective-permute-done.4.pack_other
  103.8 0.1 shard_map.103
  103.9 3.4 %shard_map.104 = (bf16[1,4096,256]{2,1,0:T(8,128)(2,1)}, bf16[1,256,4096]{2,1,0:T(8,128)(2,1)}) custom-call(bf16[2,4096]{1,0:T(2,128)(2,1)S(1)} %get-tuple-element.67.slot_in, bf16[2,256]{1,0:T(2,128)(2,1)S(1)} %get-tuple-element.68.pre_grad, bf16[2,256]{1,0:T(2,128)(2,1)S(1)} %get-tuple-element.69.hidden, bf16[2,4096]{1,0:T(2,128)(2,1)S(1)} %get-tuple-element.70.out_grad), custom_call_target="tpu_custom_call" | custom-call | flops 8388608 | bytes 4194304 | tf_op jit(solution)/shard_map/pallas_call | solution.py:266
  107.3 1.4 %convolution_convert_fusion.1.refs_0_ = bf16[128,4096]{1,0:T(8,128)(2,1)} fusion(bf16[64,128]{1,0:T(8,128)(2,1)S(1)} %get-tuple-element.62, bf16[64,4096]{1,0:T(8,128)(2,1)S(1)} %get-tuple-element.63), kind=kOutput, calls=%fused_computation.1 | convolution fusion | flops 67633152 | bytes 1589248 | tf_op jit(solution)/shard_map/dot_general | solution.py:18
  108.7 1.4 %convolution_convert_fusion.refs_1_ = bf16[128,4096]{1,0:T(8,128)(2,1)} fusion(bf16[128,128]{1,0:T(8,128)(2,1)S(1)} %get-tuple-element.64, bf16[128,4096]{1,0:T(8,128)(2,1)S(1)} %get-tuple-element.65), kind=kOutput, calls=%fused_computation | convolution fusion | flops 134742016 | bytes 2129920 | tf_op jit(solution)/shard_map/dot_general | solution.py:18
  110.1 0.7 all-to-all-done.5.message
  110.8 0.1 shard_map.105
  110.9 8.8 %all_to_all.40.message = bf16[8,2,4096]{2,1,0:T(2,128)(2,1)S(1)} all-to-all(bf16[8,2,4096]{2,1,0:T(2,128)(2,1)S(1)} %shard_map.105), channel_id=1, replica_groups={{192,224,64,96,160,32,128,0},{193,225,65,97,161,33,129,1},{194,226,66,9..., dimensions={0} | all-to-all | bytes 262144 | tf_op jit(solution)/shard_map/all_to_all | solution.py:312
  119.7 0.6 shard_map.106
  (1 shorter events, 0.0 us)
Async XLA Ops:
  0.6 20.8 %collective-permute-start = (bf16[128,4096]{1,0:T(8,128)(2,1)}, bf16[128,4096]{1,0:T(8,128)(2,1)S(1)}, u32[]{:S(2)}, u32[]{:S(2)}) collective-permute-start(bf16[128,4096]{1,0:T(8,128)(2,1)} %tokens.1), channel_id=1, source_target_pairs={{0,1},{1,0},{2,3},{3,2},{4,5},{5,4},{6,7},{7,6},{8,9},{9,8},{10,11... | collective-permute-start | bytes 3145736 | tf_op jit(solution)/shard_map/ppermute | solution.py:306
  0.7 22.8 %collective-permute-start.2 = (bf16[128,4096]{1,0:T(8,128)(2,1)}, bf16[128,4096]{1,0:T(8,128)(2,1)S(1)}, u32[]{:S(2)}, u32[]{:S(2)}) collective-permute-start(bf16[128,4096]{1,0:T(8,128)(2,1)} %cotangent.1), channel_id=1, source_target_pairs={{0,1},{1,0},{2,3},{3,2},{4,5},{5,4},{6,7},{7,6},{8,9},{9,8},{10,11... | collective-permute-start | bytes 3145736 | tf_op jit(solution)/shard_map/ppermute | solution.py:306
  1.2 0.7 copy-start.4
  21.4 1.2 %copy-start.2 = (bf16[128,4096]{1,0:T(8,128)(2,1)S(1)}, bf16[128,4096]{1,0:T(8,128)(2,1)}, u32[]{:S(2)}) copy-start(bf16[128,4096]{1,0:T(8,128)(2,1)} %tokens.1) | copy-start | bytes 3145732
  22.6 1.2 %copy-start.3 = (bf16[128,4096]{1,0:T(8,128)(2,1)S(1)}, bf16[128,4096]{1,0:T(8,128)(2,1)}, u32[]{:S(2)}) copy-start(bf16[128,4096]{1,0:T(8,128)(2,1)} %cotangent.1) | copy-start | bytes 3145732
  23.5 1.2 %collective-permute-start.1 = (f32[2,256]{1,0:T(2,128)S(1)}, f32[2,256]{1,0:T(2,128)S(1)}, u32[]{:S(2)}, u32[]{:S(2)}) collective-permute-start(f32[2,256]{1,0:T(2,128)S(1)} %get-tuple-element.40.columns), channel_id=1, source_target_pairs={{0,1},{1,0},{2,3},{3,2},{4,5},{5,4},{6,7},{7,6},{8,9},{9,8},{10,11... | collective-permute-start | bytes 6152 | tf_op jit(solution)/shard_map/ppermute | solution.py:306
  24.7 33.1 %copy-start = (bf16[1,4096,256]{2,1,0:T(8,128)(2,1)S(1)}, bf16[1,4096,256]{2,1,0:T(8,128)(2,1)}, u32[]{:S(2)}) copy-start(bf16[1,4096,256]{2,1,0:T(8,128)(2,1)} %param.7) | copy-start | bytes 6291460
  24.7 33.1 %copy-start.1 = (bf16[1,256,4096]{2,1,0:T(8,128)(2,1)S(1)}, bf16[1,256,4096]{2,1,0:T(8,128)(2,1)}, u32[]{:S(2)}) copy-start(bf16[1,256,4096]{2,1,0:T(8,128)(2,1)} %param.8) | copy-start | bytes 6291460
  90.6 1.2 %collective-permute-start.3 = (f32[2,256]{1,0:T(2,128)S(1)}, f32[2,256]{1,0:T(2,128)S(1)}, u32[]{:S(2)}, u32[]{:S(2)}) collective-permute-start(f32[2,256]{1,0:T(2,128)S(1)} %get-tuple-element.54.columns), channel_id=1, source_target_pairs={{0,1},{1,0},{2,3},{3,2},{4,5},{5,4},{6,7},{7,6},{8,9},{9,8},{10,11... | collective-permute-start | bytes 6152 | tf_op jit(solution)/shard_map/ppermute | solution.py:306
  93.1 10.7 %collective-permute-start.4 = (bf16[32,12672]{1,0:T(8,128)(2,1)S(1)}, bf16[32,12672]{1,0:T(8,128)(2,1)S(1)}, u32[]{:S(2)}, u32[]{:S(2)}) collective-permute-start(bf16[32,12672]{1,0:T(8,128)(2,1)S(1)} %get-tuple-element.56.pack), channel_id=1, source_target_pairs={{0,1},{1,0},{2,3},{3,2},{4,5},{5,4},{6,7},{7,6},{8,9},{9,8},{10,11... | collective-permute-start | bytes 2433032 | tf_op jit(solution)/shard_map/ppermute | solution.py:306
  93.3 17.5 %all-to-all-start.5 = ((bf16[16,2,4096]{2,1,0:T(2,128)(2,1)}), bf16[16,2,4096]{2,1,0:T(2,128)(2,1)S(1)}, u32[]{:S(2)}, u32[]{:S(2)}) async-start(bf16[16,2,4096]{2,1,0:T(2,128)(2,1)} %get-tuple-element.66), calls=%async_computation.5 | async-start | bytes 524288 | tf_op jit(solution)/shard_map/all_to_all | solution.py:309
